TPU v7x, 32 devices: a whole 2x2x4 slice. The times are simulated.
32 devices in a mesh: seq: 2 (over y), rep: 4 (over z), tensor: 4 (over x, core).
Axes of the slice: x: 2, y: 2, z: 4, core: 2. Of those that a mesh axis runs over, the one named last changes fastest.
Arguments:
- key_value_rows: bfloat16 [4, 3072, 8, 256], P('rep', ('seq', 'tensor')), may hold values from -32 to 32
- queries: bfloat16 [4, 64, 64, 128], P('rep', None, 'tensor'), may hold values from -136 to 136
- w_comp: bfloat16 [2048, 512], replicated, may hold values from -0.125 to 0.125
- latent_gain: bfloat16 [512], replicated, may hold values from 0.099609375 to 1.8984375
- w_up: bfloat16 [8, 512, 256], P('tensor'), may hold values from -0.25 to 0.25
- w_out: bfloat16 [8192, 8192], P('tensor', 'seq'), may hold values from -0.0625 to 0.0625
- replica_order: int32 [4], replicated, may hold values from 0 to 3, each once
Outputs:
- decoded: bfloat16 [4, 64, 8192], P('rep', None, 'seq')
Inputs may be any that keep to these rules, and one draw needn't show every extreme that they name: replica_order is a permutation of the prompts.
All inputs are finite; a program needn't handle non-finite values.
Results may differ from a plain program's by a relative error of at most 0.01.
Values may be sent and summed in bfloat16 or wider, within the bound.
No kernel may reach another device: no remote copies, remote signals or barrier semaphores. Data moves between devices by JAX's collectives and lax.ppermute only.
A program may use at most 64 MiB of HBM per device.

v0:
```python
import itertools
import math

import jax
import jax.numpy as jnp
from jax import lax
from jax.experimental import pallas as pl
from jax.experimental.pallas import tpu as pltpu
from jax.sharding import PartitionSpec as P

BF16, F32 = jnp.bfloat16, jnp.float32
MIB = 1024 * 1024
IN_VMEM = pl.BlockSpec(memory_space=pltpu.VMEM)
IN_SMEM = pl.BlockSpec(memory_space=pltpu.SMEM)
IN_HBM = pl.BlockSpec(memory_space=pltpu.HBM)
COPIES = 8


def shape(dims, dtype):
    return jax.ShapeDtypeStruct(dims, dtype)


def call(body, name, outs, operands, vmem, scratch=(), smem_in=0, smem_out=False, hbm_in=0, cost=None):
    kept = len(operands) - hbm_in
    specs = [IN_SMEM] * smem_in + [IN_VMEM] * (kept - smem_in) + [IN_HBM] * hbm_in
    operands = [
        *operands[:kept],
        *(pltpu.with_memory_space_constraint(operand, pltpu.HBM) for operand in operands[kept:]),
    ]
    out_specs = [IN_VMEM] * len(outs)
    if smem_out:
        out_specs[-1] = IN_SMEM
    return pl.pallas_call(
        body,
        out_shape=outs,
        in_specs=specs,
        out_specs=out_specs,
        scratch_shapes=list(scratch),
        compiler_params=pltpu.CompilerParams(vmem_limit_bytes=vmem * MIB),
        cost_estimate=cost,
        name=name,
    )(*operands)


def cost(flops, moved, exps=0):
    return pl.CostEstimate(flops=int(flops), bytes_accessed=int(moved), transcendentals=int(exps))


def dot(a, b):
    return jnp.dot(a, b, preferred_element_type=F32)


def compress(rows, weight, gain):
    projected = dot(rows, weight)
    scale = lax.rsqrt(jnp.mean(projected * projected, axis=-1, keepdims=True) + 1e-06)
    return (projected * scale * gain.astype(F32)[None]).astype(BF16)


def order_index(replica_order, orders):
    table = jnp.array(orders, jnp.int32)
    match = jnp.all(table == replica_order[None], axis=1)
    return jnp.sum(jnp.where(match, lax.iota(jnp.int32, len(orders)), 0))


def route_pairs(order, back):
    return [(p, r) if back else (r, p) for r, p in enumerate(order)]


def route(value, index, orders, back):
    def branch(order):
        return lambda v: lax.ppermute(v, "rep", route_pairs(order, back))

    return lax.switch(index, [branch(o) for o in orders], value)


def shift(value, axis, hops):
    size = lax.axis_size(axis)
    return lax.ppermute(value, axis, [(i, (i + hops) % size) for i in range(size)])


def swap(value, axis, bit):
    pairs = [(i, i ^ bit) for i in range(lax.axis_size(axis))]
    return lax.ppermute(value, axis, pairs)


def cross(value, seq_core):
    pairs = [(i, i ^ (4 if i % 2 == seq_core else 2)) for i in range(8)]
    return lax.ppermute(value, ("seq", "tensor"), pairs)


def compress_kernel(chunks, *refs):
    (order_hbm, rows_hbm, weight_hbm, gain_hbm, query_hbm, latent_ref, half_ref, index_ref) = refs[:8]
    (order_ref, rows_ref, weight_ref, gain_ref, query_ref, wide, packed, sems) = refs[8:]
    tokens, groups, width = rows_ref.shape
    chunk = tokens // chunks
    copies = [pltpu.make_async_copy(order_hbm, order_ref, sems.at[0])]
    for i in range(chunks):
        at = pl.ds(i * chunk, chunk)
        copies.append(pltpu.make_async_copy(rows_hbm.at[0, at], rows_ref.at[at], sems.at[1 + i]))
    for group in range(groups):
        at = pl.ds(group * width, width)
        copies.append(
            pltpu.make_async_copy(weight_hbm.at[at], weight_ref.at[at], sems.at[1 + chunks + group])
        )
    copies.append(pltpu.make_async_copy(gain_hbm, gain_ref, sems.at[1 + chunks + groups]))
    copies.append(pltpu.make_async_copy(query_hbm.at[0], query_ref, sems.at[2 + chunks + groups]))
    for copy in copies:
        copy.start()

    copies[0].wait()
    count = order_ref.shape[0]
    index = 0
    for i in range(count):
        smaller = 0
        for j in range(i + 1, count):
            smaller = smaller + (order_ref[j] < order_ref[i]).astype(jnp.int32)
        index = index + smaller * math.factorial(count - 1 - i)
    index_ref[0] = index

    lanes = wide.shape[2]
    for i in range(chunks):
        copies[1 + i].wait()
        at = slice(i * chunk * groups, (i + 1) * chunk * groups)
        for part in range(wide.shape[0]):
            values = rows_ref[i * chunk : (i + 1) * chunk, :, part * lanes : (part + 1) * lanes]
            wide[part, at] = values.astype(F32).reshape(chunk * groups, lanes)
        for group in range(groups):
            for part in range(wide.shape[0]):
                start = group * width + part * lanes
                picked = wide[part, pl.ds(at.start + group, chunk, stride=groups), :]
                packed[i * chunk : (i + 1) * chunk, start : start + lanes] = picked.astype(BF16)
    for group in range(groups):
        copies[1 + chunks + group].wait()
    copies[1 + chunks + groups].wait()
    gain = gain_ref[...].astype(F32)[None]
    for i in range(chunks):
        at = slice(i * chunk, (i + 1) * chunk)
        projected = dot(packed[at], weight_ref[...])
        scale = lax.rsqrt(jnp.mean(projected * projected, axis=-1, keepdims=True) + 1e-06)
        latent_ref[at] = (projected * scale * gain).astype(BF16)

    copies[2 + chunks + groups].wait()
    new_count, heads, head_size = query_ref.shape
    query = query_ref[...].astype(F32)
    upper = lax.axis_index("seq") == 1
    query = jnp.where(upper, query[:, heads // 2 :], query[:, : heads // 2])
    half_ref[...] = query.reshape(half_ref.shape).astype(BF16)


def score_kernel(parts, *refs):
    latent_refs, (lift_ref, query_ref), (score_ref, value_ref, top_ref) = (
        refs[:parts],
        refs[parts : parts + 2],
        refs[parts + 2 :],
    )
    head_size = query_ref.shape[-1]
    lift = lift_ref[lax.axis_index("seq")]
    query = query_ref[...]
    top = None
    for part, latent_ref in enumerate(latent_refs):
        tokens = latent_ref.shape[0]
        at = slice(part * tokens, (part + 1) * tokens)
        lifted = dot(latent_ref[...], lift).astype(BF16)
        score = lax.dot_general(
            lifted[:, :head_size], query, (((1,), (1,)), ((), ())), preferred_element_type=F32
        )
        score_ref[at] = score
        value_ref[at] = lifted[:, head_size:]
        part_top = jnp.max(score, axis=0, keepdims=True)
        top = part_top if top is None else jnp.maximum(top, part_top)
    top_ref[...] = jnp.broadcast_to(top, top_ref.shape)


def weight_copies(own, weight_ref, held_ref, sems):
    rows = held_ref.shape[0] // COPIES
    half = lax.axis_index("seq") if own else 1 - lax.axis_index("seq")
    copies = []
    for i in range(COPIES):
        start = pl.multiple_of(half * held_ref.shape[0] + i * rows, rows)
        source = weight_ref.at[pl.ds(start, rows)]
        copies.append(
            pltpu.make_async_copy(source, held_ref.at[pl.ds(i * rows, rows)], sems.at[i])
        )
    return copies


def score_and_fetch_kernel(parts, *refs):
    *refs, held_ref, sems = refs
    copies = weight_copies(True, refs.pop(parts + 2), held_ref, sems)
    for copy in copies:
        copy.start()
    score_kernel(parts, *refs)
    for copy in copies:
        copy.wait()


def score_call(name, latents, lift, query, weight=None):
    tokens = sum(latent.shape[0] for latent in latents)
    rows, head_size = query.shape
    flops = 2 * tokens * (lift.shape[1] * lift.shape[2] + rows * head_size)
    outs = [shape((tokens, rows), F32), shape((tokens, head_size), BF16), shape((8, rows), F32)]
    operands = [*latents, lift, query]
    if weight is None:
        body = lambda *refs: score_kernel(len(latents), *refs)
        return call(body, name, outs, operands, 16, cost=cost(flops, 6 * tokens * rows))
    held = (weight.shape[0] // 2, weight.shape[1])
    return call(
        lambda *refs: score_and_fetch_kernel(len(latents), *refs),
        name,
        [*outs, pltpu.VMEM(held, weight.dtype)],
        [*operands, weight],
        16,
        scratch=[pltpu.SemaphoreType.DMA((COPIES,))],
        hbm_in=1,
        cost=cost(flops, 2 * held[0] * held[1]),
    )


def attend_kernel(new_count, block, *refs):
    (*score_refs, out_ref, turned) = refs
    triples = [score_refs[i : i + 3] for i in range(0, len(score_refs), 3)]
    head_size = triples[0][1].shape[-1]
    coef = head_size ** (-0.5) * math.log2(math.e)
    top = triples[0][2][:1]
    for triple in triples[1:]:
        top = jnp.maximum(top, triple[2][:1])
    total = jnp.zeros_like(top)
    summed = jnp.zeros((head_size, top.shape[1]), F32)
    for score_ref, value_ref, _ in triples:
        for start in range(0, score_ref.shape[0], block):
            at = slice(start, start + block)
            expo = jnp.exp2((score_ref[at] - top) * coef)
            total += jnp.sum(expo, axis=0, keepdims=True)
            summed += lax.dot_general(
                value_ref[at], expo.astype(BF16), (((0,), (0,)), ((), ())), preferred_element_type=F32
            )
    turned[...] = (summed / total).T
    heads = turned.shape[0] // new_count
    for head in range(heads):
        out_ref[:, head * head_size : (head + 1) * head_size] = turned[
            pl.ds(head, new_count, stride=heads), :
        ].astype(BF16)


def project_kernel(tile, rows_ref, weight_ref, all_ref, out_ref, held_ref, sems):
    copies = weight_copies(False, all_ref, held_ref, sems)
    for copy in copies:
        copy.start()
    rows = rows_ref[...]
    width = out_ref.shape[2]
    for part in range(out_ref.shape[0]):
        for column in range(0, width, tile):
            at = part * width + column
            out_ref[part, :, column : column + tile] = dot(
                rows, weight_ref[:, at : at + tile]
            )
    for copy in copies:
        copy.wait()


def project_more_kernel(tile, own, rows_ref, weight_ref, before_ref, *refs):
    out_ref = refs[-1]
    core = lax.axis_index("tensor") % 2
    part = core if own else 1 - core
    rows = rows_ref[...]
    width = out_ref.shape[1]
    for column in range(0, width, tile):
        at = pl.multiple_of(part * width + column, tile)
        value = before_ref[part, :, column : column + tile] + dot(
            rows, weight_ref[:, pl.ds(at, tile)]
        )
        out_ref[:, column : column + tile] = value


def square_shards(key_value_rows, queries, w_comp, latent_gain, w_up, w_out, replica_order):
    orders = list(itertools.permutations(range(lax.axis_size("rep"))))
    tensor_at = lax.axis_index("tensor")
    core_at, chip_at = tensor_at % 2, tensor_at // 2
    _, new_count, heads, head_size = queries.shape
    _, tokens, all_groups, width = key_value_rows.shape
    latent_width = w_comp.shape[1]
    rows = heads // 2 * new_count

    chunks = 3 if tokens % 48 == 0 else 1
    latent, query, index = call(
        lambda *refs: compress_kernel(chunks, *refs),
        "compress",
        [shape((tokens, latent_width), BF16), shape((rows, head_size), BF16), shape((1,), jnp.int32)],
        [replica_order, key_value_rows, w_comp, latent_gain, queries],
        16,
        scratch=[
            pltpu.SMEM(replica_order.shape, jnp.int32),
            pltpu.VMEM(key_value_rows.shape[1:], BF16),
            pltpu.VMEM(w_comp.shape, BF16),
            pltpu.VMEM(latent_gain.shape, BF16),
            pltpu.VMEM(queries.shape[1:], BF16),
            pltpu.VMEM((width // 128, tokens * all_groups, 128), F32),
            pltpu.VMEM((tokens, all_groups * width), BF16),
            pltpu.SemaphoreType.DMA((3 + chunks + all_groups,)),
        ],
        hbm_in=5,
        smem_out=True,
        cost=cost(2 * tokens * all_groups * width * latent_width, 2 * tokens * all_groups * width),
    )

    def branch(order):
        def run(latent, query):
            return (
                cross(latent, 0),
                cross(latent, 1),
                swap(latent, "tensor", 1),
                lax.ppermute(query, "rep", route_pairs(order, False)),
            )

        return run

    near, far, beside, query = lax.switch(index[0], [branch(o) for o in orders], latent, query)
    corner = cross(near, 1)
    near_beside = swap(near, "tensor", 1)
    far_beside = swap(far, "tensor", 1)
    *first, held = score_call("score_chip", [latent, beside], w_up, query, w_out)
    *second, = score_call("score_next", [near, near_beside, far, far_beside], w_up, query)
    corner, first[2], second[2] = lax.optimization_barrier((corner, first[2], second[2]))
    corner_beside = swap(corner, "tensor", 1)
    third = score_call("score_corner", [corner, corner_beside], w_up, query)
    depth = rows // new_count * head_size
    (attended,) = call(
        lambda *refs: attend_kernel(new_count, tokens, *refs),
        "attend",
        [shape((new_count, depth), BF16)],
        [*first, *second, *third],
        16,
        scratch=[pltpu.VMEM((rows, head_size), F32)],
        cost=cost(2 * 8 * tokens * rows * head_size, 8 * tokens * rows * 4, 8 * tokens * rows),
    )

    attended_other = swap(attended, "seq", 1)
    columns = w_out.shape[1]
    tile = min(512, columns // 2)
    partial, held_other = call(
        lambda *refs: project_kernel(tile, *refs),
        "project",
        [shape((2, new_count, columns // 2), F32), pltpu.VMEM(held.shape, held.dtype)],
        [attended, held, w_out],
        12,
        scratch=[pltpu.SemaphoreType.DMA((COPIES,))],
        hbm_in=1,
        cost=cost(2 * new_count * depth * columns, 2 * depth * columns),
    )

    def project_more(own, name):
        return call(
            lambda *refs: project_more_kernel(tile, own, *refs),
            name,
            [shape((new_count, columns // 2), F32)],
            [attended_other, held_other, partial],
            12,
            cost=cost(new_count * depth * columns, depth * columns),
        )[0]

    sent = swap(project_more(False, "project_sent"), "tensor", 1)
    half = project_more(True, "project_own") + sent
    quarter = half.shape[1] // 2
    low, high = half[:, :quarter], half[:, quarter:]
    upper = chip_at == 1
    arrived = swap(jnp.where(upper, low, high), "tensor", 2)
    summed = (jnp.where(upper, high, low) + arrived).astype(BF16)

    def reply(order):
        def run(value):
            pairs = [(p * 4 + t, r * 4 + t) for r, p in enumerate(order) for t in range(4)]
            crossed = [(source, target ^ 2) for source, target in pairs]
            axes = ("rep", "tensor")
            return lax.ppermute(value, axes, pairs), lax.ppermute(value, axes, crossed)

        return run

    summed, summed_across = lax.switch(index[0], [reply(o) for o in orders], summed)
    half = jnp.where(
        upper,
        jnp.concatenate([summed_across, summed], axis=1),
        jnp.concatenate([summed, summed_across], axis=1),
    )
    half_beside = swap(half, "tensor", 1)
    whole = jnp.where(
        core_at == 1,
        jnp.concatenate([half_beside, half], axis=1),
        jnp.concatenate([half, half_beside], axis=1),
    )
    return whole[None]


def shards(key_value_rows, queries, w_comp, latent_gain, w_up, w_out, replica_order):
    orders = list(itertools.permutations(range(lax.axis_size("rep"))))
    index = order_index(replica_order, orders)
    query = route(queries[0], index, orders, False)
    rows = key_value_rows[0]
    latent = compress(rows.reshape(rows.shape[0], -1), w_comp, latent_gain)
    latent = lax.all_gather(latent, "tensor", axis=0, tiled=True)
    groups = w_up.shape[0]
    lifted = jnp.einsum("tf,gfy->tgy", latent, w_up, preferred_element_type=F32).astype(BF16)
    head_size = query.shape[-1]
    new_count = query.shape[0]
    keys = lifted[..., :head_size]
    values = lifted[..., head_size:]
    grouped_heads = query.reshape(new_count, groups, -1, head_size)
    scores = jnp.einsum(
        "nghd,tgd->nght", grouped_heads, keys, preferred_element_type=F32
    ) * head_size ** (-0.5)
    top = lax.pmax(jnp.max(scores, axis=-1), "seq")
    expo = jnp.exp(scores - top[..., None])
    total = jnp.sum(expo, axis=-1)
    summed = jnp.einsum("nght,tgd->nghd", expo.astype(BF16), values, preferred_element_type=F32)
    summed, total = lax.psum((summed, total), "seq")
    attended = (summed / total[..., None]).astype(BF16).reshape(new_count, -1)
    attended = route(attended, index, orders, True)
    return lax.psum(dot(attended, w_out), "tensor").astype(BF16)[None]


def solution(mesh):
    placed = (
        P("rep", ("seq", "tensor"), None, None),
        P("rep", None, "tensor", None),
        P(),
        P(),
        P("tensor", None, None),
        P("tensor", "seq"),
        P(),
    )
    square = mesh.shape["seq"] == 2 and mesh.shape["tensor"] == 4
    return jax.shard_map(
        square_shards if square else shards,
        mesh=mesh,
        in_specs=placed,
        out_specs=P("rep", None, "seq"),
        check_vma=False,
    )
```

profile of v0, /device:TPU:0, one launch (start us, length us, event | category | flops | bytes accessed | tf_op | source)
XLA Modules:
  0.0 77.2 jit_solution(13685988682792603635)
XLA Ops:
  0.0 0.0 copy-start.2
  0.0 3.8 %compress.1 = (bf16[384,512]{1,0:T(8,128)(2,1)S(1)}, bf16[512,128]{1,0:T(8,128)(2,1)S(1)}, s32[1]{0:T(128)}) custom-call(s32[4]{0:T(128)} %refs_0_.1, bf16[1,384,8,256]{3,2,1,0:T(8,128)(2,1)} %refs_1_.1, bf16[2048,512]{1,0:T(8,128)(2,1)} %refs_2_.4, bf16[512]{0:T(512)(128)(2,1)} %refs_3_.1, bf16[1,64,16,128]{3,2,1,0:T(8,128)(2,1)} %refs_4_.3), custom_call_target="tpu_custom_call" | custom-call | flops 805306368 | bytes 1572864 | tf_op jit(solution)/shard_map/compress/pallas_call | solution.py:33
  4.4 12.7 %conditional.2 = (bf16[384,512]{1,0:T(8,128)(2,1)}, bf16[384,512]{1,0:T(8,128)(2,1)}, bf16[384,512]{1,0:T(8,128)(2,1)}, bf16[512,128]{1,0:T(8,128)(2,1)}) conditional(s32[]{:T(128)} %bitcast, (bf16[384,512]{1,0:T(8,128)(2,1)S(1)}, bf16[512,128]{1,0:T(8,128)(2,1)S(1)}) %tuple.198, (bf16[384,512]{1,0:T(8,128)(2,1)S(1)}, ...), branch_computations={%region_0.1_spmd, %region_1.2_spmd, %region_2.3_spmd, %region_3.4_... | conditional | bytes 5243072 | solution.py:317
  4.4 3.0 %collective-permute-start.48 = (bf16[384,512]{1,0:T(8,128)(2,1)S(1)}, bf16[384,512]{1,0:T(8,128)(2,1)}, u32[]{:S(2)}, u32[]{:S(2)}) collective-permute-start(bf16[384,512]{1,0:T(8,128)(2,1)S(1)} %get-tuple-element.149), channel_id=1, source_target_pairs={{0,16},{1,3},{2,18},{3,1},{16,0},{17,19},{18,2},{19,17},{4,20},{5,... | collective-permute-start | bytes 1179656 | tf_op jit(solution)/shard_map/cond/branch_12_fun/ppermute | solution.py:88
  7.5 1.5 %collective-permute-start.49 = (bf16[384,512]{1,0:T(8,128)(2,1)S(1)}, bf16[384,512]{1,0:T(8,128)(2,1)}, u32[]{:S(2)}, u32[]{:S(2)}) collective-permute-start(bf16[384,512]{1,0:T(8,128)(2,1)S(1)} %get-tuple-element.149), channel_id=1, source_target_pairs={{0,2},{1,17},{2,0},{3,19},{16,18},{17,1},{18,16},{19,3},{4,6},{5,2... | collective-permute-start | bytes 1179656 | tf_op jit(solution)/shard_map/cond/branch_12_fun/ppermute | solution.py:88
  9.0 0.0 collective-permute-start.50
  9.0 4.5 %collective-permute-start.51 = (bf16[512,128]{1,0:T(8,128)(2,1)S(1)}, bf16[512,128]{1,0:T(8,128)(2,1)}, u32[]{:S(2)}, u32[]{:S(2)}) collective-permute-start(bf16[512,128]{1,0:T(8,128)(2,1)S(1)} %get-tuple-element.150), channel_id=1, source_target_pairs={{0,8},{4,0},{8,4},{12,12},{1,9},{5,1},{9,5},{13,13},{2,10},{6,2},{... | collective-permute-start | bytes 393224 | tf_op jit(solution)/shard_map/cond/branch_12_fun/ppermute | solution.py:312
  13.5 3.4 %collective-permute-done.51 = bf16[512,128]{1,0:T(8,128)(2,1)} collective-permute-done((bf16[512,128]{1,0:T(8,128)(2,1)S(1)}, bf16[512,128]{1,0:T(8,128)(2,1)}, u32[]{:S(2)}, u32[]{:S(2)}) %collective-permute-start.51) | collective-permute-done | bytes 131104 | tf_op jit(solution)/shard_map/cond/branch_12_fun/ppermute | solution.py:312
  16.9 0.2 collective-permute-done.48
  17.0 0.0 collective-permute-done.49
  17.0 0.0 collective-permute-done.50
  17.1 0.3 collective-permute-start.145
  17.4 0.3 collective-permute-start.146
  17.7 1.4 %collective-permute-start.144 = (bf16[384,512]{1,0:T(8,128)(2,1)}, bf16[384,512]{1,0:T(8,128)(2,1)S(1)}, u32[]{:S(2)}, u32[]{:S(2)}) collective-permute-start(bf16[384,512]{1,0:T(8,128)(2,1)} %get-tuple-element.204.refs_0_), channel_id=1, source_target_pairs={{0,2},{1,17},{2,0},{3,19},{16,18},{17,1},{18,16},{19,3},{4,6},{5,2... | collective-permute-start | bytes 1179656 | tf_op jit(solution)/shard_map/ppermute | solution.py:88
  19.1 0.0 copy-done.2
  19.1 5.1 %score_chip.1 = (f32[768,512]{1,0:T(8,128)S(1)}, bf16[768,128]{1,0:T(8,128)(2,1)S(1)}, f32[8,512]{1,0:T(8,128)S(1)}, bf16[1024,4096]{1,0:T(8,128)(2,1)S(1)}) custom-call(bf16[384,512]{1,0:T(8,128)(2,1)S(1)} %get-tuple-element.198.refs_0_, bf16[384,512]{1,0:T(8,128)(2,1)} %get-tuple-element.200.refs_1_, bf16[2,512,256]{2,1,0:T(8,128)(2,1)S(1)} %copy-done.2, ...), custom_call_target="tpu_custom_call" | custom-call | flops 301989888 | bytes 8388608 | tf_op jit(solution)/shard_map/score_chip/pallas_call | solution.py:33
  24.1 0.0 collective-permute-done.145.refs_1_
  24.1 0.0 collective-permute-done.146.refs_3_
  24.2 2.3 %score_next.1 = (f32[1536,512]{1,0:T(8,128)S(1)}, bf16[1536,128]{1,0:T(8,128)(2,1)S(1)}, f32[8,512]{1,0:T(8,128)S(1)}) custom-call(bf16[384,512]{1,0:T(8,128)(2,1)} %get-tuple-element.204.refs_0_, bf16[384,512]{1,0:T(8,128)(2,1)S(1)} %collective-permute-done.145.refs_1_, bf16[384,512]{1,0:T(8,128)(2,1)} %get-tuple-element.206.refs_2_, ...), custom_call_target="tpu_custom_call" | custom-call | flops 603979776 | bytes 4718592 | tf_op jit(solution)/shard_map/score_next/pallas_call | solution.py:33
  26.5 0.0 collective-permute-done.144.refs_0_
  26.5 0.9 %collective-permute-start.147 = (bf16[384,512]{1,0:T(8,128)(2,1)S(1)}, bf16[384,512]{1,0:T(8,128)(2,1)S(1)}, u32[]{:S(2)}, u32[]{:S(2)}) collective-permute-start(bf16[384,512]{1,0:T(8,128)(2,1)S(1)} %collective-permute-done.144.refs_0_), channel_id=1, source_target_pairs={{0,1},{1,0},{2,3},{3,2},{4,5},{5,4},{6,7},{7,6},{8,9},{9,8},{10,11... | collective-permute-start | bytes 1179656 | tf_op jit(solution)/shard_map/ppermute | solution.py:83
  27.4 1.3 %collective-permute-done.147.refs_1_ = bf16[384,512]{1,0:T(8,128)(2,1)S(1)} collective-permute-done((bf16[384,512]{1,0:T(8,128)(2,1)S(1)}, bf16[384,512]{1,0:T(8,128)(2,1)S(1)}, u32[]{:S(2)}, u32[]{:S(2)}) %collective-permute-start.147) | collective-permute-done | bytes 393248 | tf_op jit(solution)/shard_map/ppermute | solution.py:83
  28.7 1.7 %score_corner.1 = (f32[768,512]{1,0:T(8,128)S(1)}, bf16[768,128]{1,0:T(8,128)(2,1)S(1)}, f32[8,512]{1,0:T(8,128)S(1)}) custom-call(bf16[384,512]{1,0:T(8,128)(2,1)S(1)} %collective-permute-done.144.refs_0_, bf16[384,512]{1,0:T(8,128)(2,1)S(1)} %collective-permute-done.147.refs_1_, bf16[2,512,256]{2,1,0:T(8,128)(2,1)S(1)} %copy-done.2, ...), custom_call_target="tpu_custom_call" | custom-call | flops 301989888 | bytes 2359296 | tf_op jit(solution)/shard_map/score_corner/pallas_call | solution.py:33
  30.4 1.4 %attend.1.refs_0_ = bf16[64,1024]{1,0:T(8,128)(2,1)S(1)} custom-call(f32[768,512]{1,0:T(8,128)S(1)} %get-tuple-element.202.refs_0_, bf16[768,128]{1,0:T(8,128)(2,1)S(1)} %get-tuple-element.203.refs_1_, f32[8,512]{1,0:T(8,128)S(1)} %get-tuple-element.208.refs_2_, f32[1536,512]{1,0:T(8,128)S(1)} %get-tuple-element.209.refs_3_, ...), custom_call_target="tpu_custom_call" | custom-call | flops 402653184 | bytes 6291456 | tf_op jit(solution)/shard_map/attend/pallas_call | solution.py:33
  31.9 5.3 %collective-permute-start.148 = (bf16[64,1024]{1,0:T(8,128)(2,1)S(1)}, bf16[64,1024]{1,0:T(8,128)(2,1)S(1)}, u32[]{:S(2)}, u32[]{:S(2)}) collective-permute-start(bf16[64,1024]{1,0:T(8,128)(2,1)S(1)} %attend.1.refs_0_), channel_id=1, source_target_pairs={{0,16},{16,0},{1,17},{17,1},{2,18},{18,2},{3,19},{19,3},{4,20},{20... | collective-permute-start | bytes 393224 | tf_op jit(solution)/shard_map/ppermute | solution.py:83
  37.1 4.9 %project.1 = (f32[2,64,2048]{2,1,0:T(8,128)S(1)}, bf16[1024,4096]{1,0:T(8,128)(2,1)S(1)}) custom-call(bf16[64,1024]{1,0:T(8,128)(2,1)S(1)} %attend.1.refs_0_, bf16[1024,4096]{1,0:T(8,128)(2,1)S(1)} %get-tuple-element.216.refs_1_, bf16[2048,4096]{1,0:T(8,128)(2,1)} %refs_2_.7), custom_call_target="tpu_custom_call" | custom-call | flops 536870912 | bytes 8388608 | tf_op jit(solution)/shard_map/project/pallas_call | solution.py:33
  42.0 0.0 copy-start
  42.0 0.8 %collective-permute-done.148.refs_0_ = bf16[64,1024]{1,0:T(8,128)(2,1)S(1)} collective-permute-done((bf16[64,1024]{1,0:T(8,128)(2,1)S(1)}, bf16[64,1024]{1,0:T(8,128)(2,1)S(1)}, u32[]{:S(2)}, u32[]{:S(2)}) %collective-permute-start.148) | collective-permute-done | bytes 131104 | tf_op jit(solution)/shard_map/ppermute | solution.py:83
  42.8 0.8 %project_sent.1 = f32[64,2048]{1,0:T(8,128)S(1)} custom-call(bf16[64,1024]{1,0:T(8,128)(2,1)S(1)} %collective-permute-done.148.refs_0_, bf16[1024,4096]{1,0:T(8,128)(2,1)S(1)} %get-tuple-element.217.refs_1_, f32[2,64,2048]{2,1,0:T(8,128)S(1)} %get-tuple-element.218.refs_2_), custom_call_target="tpu_custom_call" | custom-call | flops 268435456 | bytes 4194304 | tf_op jit(solution)/shard_map/project_sent/pallas_call | solution.py:33
  43.7 1.8 %copy-done = bf16[1024,4096]{1,0:T(8,128)(2,1)} copy-done((bf16[1024,4096]{1,0:T(8,128)(2,1)}, bf16[1024,4096]{1,0:T(8,128)(2,1)S(1)}, u32[]{:S(2)}) %copy-start) | copy-done | bytes 8388632
  45.4 0.4 collective-permute-start.149
  45.8 0.0 copy-start.1
  45.8 3.4 %copy-done.1 = bf16[1024,4096]{1,0:T(8,128)(2,1)S(1)} copy-done((bf16[1024,4096]{1,0:T(8,128)(2,1)S(1)}, bf16[1024,4096]{1,0:T(8,128)(2,1)}, u32[]{:S(2)}) %copy-start.1) | copy-done | bytes 8388632
  49.2 0.8 %project_own.1 = f32[64,2048]{1,0:T(8,128)S(1)} custom-call(bf16[64,1024]{1,0:T(8,128)(2,1)S(1)} %collective-permute-done.148.refs_0_, bf16[1024,4096]{1,0:T(8,128)(2,1)S(1)} %copy-done.1, f32[2,64,2048]{2,1,0:T(8,128)S(1)} %get-tuple-element.218.refs_2_), custom_call_target="tpu_custom_call" | custom-call | flops 268435456 | bytes 4194304 | tf_op jit(solution)/shard_map/project_own/pallas_call | solution.py:33
  50.0 0.0 collective-permute-done.149
  50.1 0.1 add.12
  50.2 1.7 %collective-permute-start.150 = (f32[64,1024]{1,0:T(8,128)S(1)}, f32[64,1024]{1,0:T(8,128)S(1)}, u32[]{:S(2)}, u32[]{:S(2)}) collective-permute-start(f32[64,1024]{1,0:T(8,128)S(1)} %slice_select_fusion), channel_id=1, source_target_pairs={{0,2},{1,3},{2,0},{3,1},{4,6},{5,7},{6,4},{7,5},{8,10},{9,11},{10,... | collective-permute-start | bytes 786440 | tf_op jit(solution)/shard_map/ppermute | solution.py:83
  51.9 6.8 %collective-permute-done.150 = f32[64,1024]{1,0:T(8,128)S(1)} collective-permute-done((f32[64,1024]{1,0:T(8,128)S(1)}, f32[64,1024]{1,0:T(8,128)S(1)}, u32[]{:S(2)}, u32[]{:S(2)}) %collective-permute-start.150) | collective-permute-done | bytes 262176 | tf_op jit(solution)/shard_map/ppermute | solution.py:83
  58.8 14.8 %conditional.3 = (bf16[64,1024]{1,0:T(8,128)(2,1)}, bf16[64,1024]{1,0:T(8,128)(2,1)}) conditional(s32[]{:T(128)} %bitcast, bf16[64,1024]{1,0:T(8,128)(2,1)S(1)} %add_convert_fusion, bf16[64,1024]{1,0:T(8,128)(2,1)S(1)} %add_convert_fusion, bf16[64,1024]{1,0:T(8,128)(2,1)S(1)} %add_convert_fusion, ...), branch_computations={%region_24.25_spmd, %region_25.26_spmd, %region_26.27_spmd, %regio... | conditional | bytes 1048672 | solution.py:378
  58.8 3.7 %collective-permute-start.120 = (bf16[64,1024]{1,0:T(8,128)(2,1)S(1)}, bf16[64,1024]{1,0:T(8,128)(2,1)}, u32[]{:S(2)}, u32[]{:S(2)}) collective-permute-start(bf16[64,1024]{1,0:T(8,128)(2,1)S(1)} %param.36), channel_id=1, source_target_pairs={{8,0},{9,1},{10,2},{11,3},{0,4},{1,5},{2,6},{3,7},{4,8},{5,9},{6,1... | collective-permute-start | bytes 393224 | tf_op jit(solution)/shard_map/cond/branch_12_fun/ppermute | solution.py:374
  62.5 3.5 %collective-permute-start.121 = (bf16[64,1024]{1,0:T(8,128)(2,1)S(1)}, bf16[64,1024]{1,0:T(8,128)(2,1)}, u32[]{:S(2)}, u32[]{:S(2)}) collective-permute-start(bf16[64,1024]{1,0:T(8,128)(2,1)S(1)} %param.36), channel_id=1, source_target_pairs={{8,2},{9,3},{10,0},{11,1},{0,6},{1,7},{2,4},{3,5},{4,10},{5,11},{6... | collective-permute-start | bytes 393224 | tf_op jit(solution)/shard_map/cond/branch_12_fun/ppermute | solution.py:374
  66.0 0.7 collective-permute-done.120
  66.7 6.9 %collective-permute-done.121 = bf16[64,1024]{1,0:T(8,128)(2,1)} collective-permute-done((bf16[64,1024]{1,0:T(8,128)(2,1)S(1)}, bf16[64,1024]{1,0:T(8,128)(2,1)}, u32[]{:S(2)}, u32[]{:S(2)}) %collective-permute-start.121) | collective-permute-done | bytes 131104 | tf_op jit(solution)/shard_map/cond/branch_12_fun/ppermute | solution.py:374
  73.6 1.2 %maximum_select_fusion.1 = bf16[64,2048]{1,0:T(8,128)(2,1)S(1)} fusion(bf16[64,1024]{1,0:T(8,128)(2,1)} %get-tuple-element.220, bf16[64,1024]{1,0:T(8,128)(2,1)} %get-tuple-element.219, pred[]{:T(512)S(6)} %eq.9), kind=kLoop, calls=%fused_computation.1 | loop fusion | flops 1179648 | bytes 524289 | tf_op jit(solution)/shard_map/jit(_where)/select_n | solution.py:379
  74.7 0.1 collective-permute-start.151
  74.8 1.5 %collective-permute-done.151 = bf16[64,2048]{1,0:T(8,128)(2,1)S(1)} collective-permute-done((bf16[64,2048]{1,0:T(8,128)(2,1)S(1)}, bf16[64,2048]{1,0:T(8,128)(2,1)S(1)}, u32[]{:S(2)}, u32[]{:S(2)}) %collective-permute-start.151) | collective-permute-done | bytes 262176 | tf_op jit(solution)/shard_map/ppermute | solution.py:83
  76.3 0.9 %maximum_select_fusion = bf16[1,64,4096]{2,1,0:T(8,128)(2,1)} fusion(bf16[1,64,2048]{2,1,0:T(8,128)(2,1)S(1)} %bitcast.3, bf16[1,64,2048]{2,1,0:T(8,128)(2,1)S(1)} %bitcast.4, pred[]{:T(512)S(6)} %eq.8), kind=kLoop, calls=%fused_computation | loop fusion | flops 2359296 | bytes 1048577 | tf_op jit(solution)/shard_map/jit(_where)/select_n | solution.py:385
  (2 shorter events, 0.1 us)
Async XLA Ops:
  0.0 19.1 %copy-start.2 = (bf16[2,512,256]{2,1,0:T(8,128)(2,1)S(1)}, bf16[2,512,256]{2,1,0:T(8,128)(2,1)}, u32[]{:S(2)}) copy-start(bf16[2,512,256]{2,1,0:T(8,128)(2,1)} %refs_2_.6) | copy-start | bytes 1572868
  4.4 12.6 %collective-permute-start.48 = (bf16[384,512]{1,0:T(8,128)(2,1)S(1)}, bf16[384,512]{1,0:T(8,128)(2,1)}, u32[]{:S(2)}, u32[]{:S(2)}) collective-permute-start(bf16[384,512]{1,0:T(8,128)(2,1)S(1)} %get-tuple-element.149), channel_id=1, source_target_pairs={{0,16},{1,3},{2,18},{3,1},{16,0},{17,19},{18,2},{19,17},{4,20},{5,... | collective-permute-start | bytes 1179656 | tf_op jit(solution)/shard_map/cond/branch_12_fun/ppermute | solution.py:88
  7.5 9.6 %collective-permute-start.49 = (bf16[384,512]{1,0:T(8,128)(2,1)S(1)}, bf16[384,512]{1,0:T(8,128)(2,1)}, u32[]{:S(2)}, u32[]{:S(2)}) collective-permute-start(bf16[384,512]{1,0:T(8,128)(2,1)S(1)} %get-tuple-element.149), channel_id=1, source_target_pairs={{0,2},{1,17},{2,0},{3,19},{16,18},{17,1},{18,16},{19,3},{4,6},{5,2... | collective-permute-start | bytes 1179656 | tf_op jit(solution)/shard_map/cond/branch_12_fun/ppermute | solution.py:88
  9.0 8.1 %collective-permute-start.50 = (bf16[384,512]{1,0:T(8,128)(2,1)S(1)}, bf16[384,512]{1,0:T(8,128)(2,1)}, u32[]{:S(2)}, u32[]{:S(2)}) collective-permute-start(bf16[384,512]{1,0:T(8,128)(2,1)S(1)} %get-tuple-element.149), channel_id=1, source_target_pairs={{0,1},{1,0},{2,3},{3,2},{4,5},{5,4},{6,7},{7,6},{8,9},{9,8},{10,11... | collective-permute-start | bytes 1179656 | tf_op jit(solution)/shard_map/cond/branch_12_fun/ppermute | solution.py:83
  9.0 7.9 %collective-permute-start.51 = (bf16[512,128]{1,0:T(8,128)(2,1)S(1)}, bf16[512,128]{1,0:T(8,128)(2,1)}, u32[]{:S(2)}, u32[]{:S(2)}) collective-permute-start(bf16[512,128]{1,0:T(8,128)(2,1)S(1)} %get-tuple-element.150), channel_id=1, source_target_pairs={{0,8},{4,0},{8,4},{12,12},{1,9},{5,1},{9,5},{13,13},{2,10},{6,2},{... | collective-permute-start | bytes 393224 | tf_op jit(solution)/shard_map/cond/branch_12_fun/ppermute | solution.py:312
  17.1 7.0 %collective-permute-start.145 = (bf16[384,512]{1,0:T(8,128)(2,1)}, bf16[384,512]{1,0:T(8,128)(2,1)S(1)}, u32[]{:S(2)}, u32[]{:S(2)}) collective-permute-start(bf16[384,512]{1,0:T(8,128)(2,1)} %get-tuple-element.204.refs_0_), channel_id=1, source_target_pairs={{0,1},{1,0},{2,3},{3,2},{4,5},{5,4},{6,7},{7,6},{8,9},{9,8},{10,11... | collective-permute-start | bytes 1179656 | tf_op jit(solution)/shard_map/ppermute | solution.py:83
  17.4 6.8 %collective-permute-start.146 = (bf16[384,512]{1,0:T(8,128)(2,1)}, bf16[384,512]{1,0:T(8,128)(2,1)S(1)}, u32[]{:S(2)}, u32[]{:S(2)}) collective-permute-start(bf16[384,512]{1,0:T(8,128)(2,1)} %get-tuple-element.206.refs_2_), channel_id=1, source_target_pairs={{0,1},{1,0},{2,3},{3,2},{4,5},{5,4},{6,7},{7,6},{8,9},{9,8},{10,11... | collective-permute-start | bytes 1179656 | tf_op jit(solution)/shard_map/ppermute | solution.py:83
  17.7 8.8 %collective-permute-start.144 = (bf16[384,512]{1,0:T(8,128)(2,1)}, bf16[384,512]{1,0:T(8,128)(2,1)S(1)}, u32[]{:S(2)}, u32[]{:S(2)}) collective-permute-start(bf16[384,512]{1,0:T(8,128)(2,1)} %get-tuple-element.204.refs_0_), channel_id=1, source_target_pairs={{0,2},{1,17},{2,0},{3,19},{16,18},{17,1},{18,16},{19,3},{4,6},{5,2... | collective-permute-start | bytes 1179656 | tf_op jit(solution)/shard_map/ppermute | solution.py:88
  26.5 2.2 %collective-permute-start.147 = (bf16[384,512]{1,0:T(8,128)(2,1)S(1)}, bf16[384,512]{1,0:T(8,128)(2,1)S(1)}, u32[]{:S(2)}, u32[]{:S(2)}) collective-permute-start(bf16[384,512]{1,0:T(8,128)(2,1)S(1)} %collective-permute-done.144.refs_0_), channel_id=1, source_target_pairs={{0,1},{1,0},{2,3},{3,2},{4,5},{5,4},{6,7},{7,6},{8,9},{9,8},{10,11... | collective-permute-start | bytes 1179656 | tf_op jit(solution)/shard_map/ppermute | solution.py:83
  31.9 11.0 %collective-permute-start.148 = (bf16[64,1024]{1,0:T(8,128)(2,1)S(1)}, bf16[64,1024]{1,0:T(8,128)(2,1)S(1)}, u32[]{:S(2)}, u32[]{:S(2)}) collective-permute-start(bf16[64,1024]{1,0:T(8,128)(2,1)S(1)} %attend.1.refs_0_), channel_id=1, source_target_pairs={{0,16},{16,0},{1,17},{17,1},{2,18},{18,2},{3,19},{19,3},{4,20},{20... | collective-permute-start | bytes 393224 | tf_op jit(solution)/shard_map/ppermute | solution.py:83
  42.0 3.4 %copy-start = (bf16[1024,4096]{1,0:T(8,128)(2,1)}, bf16[1024,4096]{1,0:T(8,128)(2,1)S(1)}, u32[]{:S(2)}) copy-start(bf16[1024,4096]{1,0:T(8,128)(2,1)S(1)} %get-tuple-element.217.refs_1_) | copy-start | bytes 25165828
  45.4 4.6 %collective-permute-start.149 = (f32[64,2048]{1,0:T(8,128)S(1)}, f32[64,2048]{1,0:T(8,128)S(1)}, u32[]{:S(2)}, u32[]{:S(2)}) collective-permute-start(f32[64,2048]{1,0:T(8,128)S(1)} %project_sent.1), channel_id=1, source_target_pairs={{0,1},{1,0},{2,3},{3,2},{4,5},{5,4},{6,7},{7,6},{8,9},{9,8},{10,11... | collective-permute-start | bytes 1572872 | tf_op jit(solution)/shard_map/ppermute | solution.py:83
  45.8 3.4 %copy-start.1 = (bf16[1024,4096]{1,0:T(8,128)(2,1)S(1)}, bf16[1024,4096]{1,0:T(8,128)(2,1)}, u32[]{:S(2)}) copy-start(bf16[1024,4096]{1,0:T(8,128)(2,1)} %copy-done) | copy-start | bytes 25165828
  50.2 8.6 %collective-permute-start.150 = (f32[64,1024]{1,0:T(8,128)S(1)}, f32[64,1024]{1,0:T(8,128)S(1)}, u32[]{:S(2)}, u32[]{:S(2)}) collective-permute-start(f32[64,1024]{1,0:T(8,128)S(1)} %slice_select_fusion), channel_id=1, source_target_pairs={{0,2},{1,3},{2,0},{3,1},{4,6},{5,7},{6,4},{7,5},{8,10},{9,11},{10,... | collective-permute-start | bytes 786440 | tf_op jit(solution)/shard_map/ppermute | solution.py:83
  58.8 7.9 %collective-permute-start.120 = (bf16[64,1024]{1,0:T(8,128)(2,1)S(1)}, bf16[64,1024]{1,0:T(8,128)(2,1)}, u32[]{:S(2)}, u32[]{:S(2)}) collective-permute-start(bf16[64,1024]{1,0:T(8,128)(2,1)S(1)} %param.36), channel_id=1, source_target_pairs={{8,0},{9,1},{10,2},{11,3},{0,4},{1,5},{2,6},{3,7},{4,8},{5,9},{6,1... | collective-permute-start | bytes 393224 | tf_op jit(solution)/shard_map/cond/branch_12_fun/ppermute | solution.py:374
  62.5 11.1 %collective-permute-start.121 = (bf16[64,1024]{1,0:T(8,128)(2,1)S(1)}, bf16[64,1024]{1,0:T(8,128)(2,1)}, u32[]{:S(2)}, u32[]{:S(2)}) collective-permute-start(bf16[64,1024]{1,0:T(8,128)(2,1)S(1)} %param.36), channel_id=1, source_target_pairs={{8,2},{9,3},{10,0},{11,1},{0,6},{1,7},{2,4},{3,5},{4,10},{5,11},{6... | collective-permute-start | bytes 393224 | tf_op jit(solution)/shard_map/cond/branch_12_fun/ppermute | solution.py:374
  74.7 1.6 %collective-permute-start.151 = (bf16[64,2048]{1,0:T(8,128)(2,1)S(1)}, bf16[64,2048]{1,0:T(8,128)(2,1)S(1)}, u32[]{:S(2)}, u32[]{:S(2)}) collective-permute-start(bf16[64,2048]{1,0:T(8,128)(2,1)S(1)} %maximum_select_fusion.1), channel_id=1, source_target_pairs={{0,1},{1,0},{2,3},{3,2},{4,5},{5,4},{6,7},{7,6},{8,9},{9,8},{10,11... | collective-permute-start | bytes 786440 | tf_op jit(solution)/shard_map/ppermute | solution.py:83
where the time goes:
time: 77.6 us; the launch traced here: 77.2 us
  starting transfers between devices  26.4 us (34%)
  waiting for transfers between devices  21.6 us (28%)
  Pallas kernels  20.9 us (27%)
  local copies, waits for them, and re-layouts  5.14 us (7%)
  other arithmetic  2.22 us (3%)
  between operations  0.81 us (1%)
    pallas_call x8, Pallas kernels, call(): pl.pallas_call(body, out_shape=outs, in_specs=specs, out_specs=out_specs,...  20.9 us
    ppermute x8, waiting for transfers between devices, swap(): return lax.ppermute(value, axis, pairs)  10.5 us
    ppermute x8, starting transfers between devices, swap(): return lax.ppermute(value, axis, pairs)  8.9 us
    ppermute x1, waiting for transfers between devices, run(): lax.ppermute(value, axes, crossed)  6.89 us
    ppermute x3, starting transfers between devices, cross(): return lax.ppermute(value, ('seq', 'tensor'), pairs)  5.9 us
    unnamed x6, local copies, waits for them, and re-layouts  5.14 us
    ppermute x1, starting transfers between devices, run(): lax.ppermute(query, 'rep', route_pairs(order, False))  4.48 us
    ppermute x1, starting transfers between devices, run(): lax.ppermute(value, axes, pairs)  3.65 us
  transfers between devices with their start and end apart: 14, of which 8 were waited for; matrix products, arithmetic and copies ran while one was open for 0% of the time, Pallas kernels for 17%

commit v1 on v0

--- a/solution.py
+++ b/solution.py
@@ -171,13 +171,15 @@
     top_ref[...] = jnp.broadcast_to(top, top_ref.shape)
 
 
-def weight_copies(own, weight_ref, held_ref, sems):
-    rows = held_ref.shape[0] // COPIES
+def weight_copies(own, core, weight_ref, held_ref, sems):
+    depth, columns = held_ref.shape
+    rows = depth // COPIES
     half = lax.axis_index("seq") if own else 1 - lax.axis_index("seq")
+    first = 0 if core is None else core * columns
     copies = []
     for i in range(COPIES):
-        start = pl.multiple_of(half * held_ref.shape[0] + i * rows, rows)
-        source = weight_ref.at[pl.ds(start, rows)]
+        start = pl.multiple_of(half * depth + i * rows, rows)
+        source = weight_ref.at[pl.ds(start, rows), pl.ds(pl.multiple_of(first, columns), columns)]
         copies.append(
             pltpu.make_async_copy(source, held_ref.at[pl.ds(i * rows, rows)], sems.at[i])
         )
@@ -186,7 +188,7 @@
 
 def score_and_fetch_kernel(parts, *refs):
     *refs, held_ref, sems = refs
-    copies = weight_copies(True, refs.pop(parts + 2), held_ref, sems)
+    copies = weight_copies(True, None, refs.pop(parts + 2), held_ref, sems)
     for copy in copies:
         copy.start()
     score_kernel(parts, *refs)
@@ -242,8 +244,10 @@
         ].astype(BF16)
 
 
-def project_kernel(tile, rows_ref, weight_ref, all_ref, out_ref, held_ref, sems):
-    copies = weight_copies(False, all_ref, held_ref, sems)
+def project_kernel(tile, rows_ref, weight_ref, all_ref, out_ref, sent_ref, kept_ref, sems):
+    core = lax.axis_index("tensor") % 2
+    copies = weight_copies(False, 1 - core, all_ref, sent_ref, sems.at[0])
+    copies += weight_copies(False, core, all_ref, kept_ref, sems.at[1])
     for copy in copies:
         copy.start()
     rows = rows_ref[...]
@@ -265,9 +269,8 @@
     rows = rows_ref[...]
     width = out_ref.shape[1]
     for column in range(0, width, tile):
-        at = pl.multiple_of(part * width + column, tile)
         value = before_ref[part, :, column : column + tile] + dot(
-            rows, weight_ref[:, pl.ds(at, tile)]
+            rows, weight_ref[:, column : column + tile]
         )
         out_ref[:, column : column + tile] = value
 
@@ -337,45 +340,38 @@
     attended_other = swap(attended, "seq", 1)
     columns = w_out.shape[1]
     tile = min(512, columns // 2)
-    partial, held_other = call(
+    half_shape = (held.shape[0], held.shape[1] // 2)
+    partial, held_sent, held_kept = call(
         lambda *refs: project_kernel(tile, *refs),
         "project",
-        [shape((2, new_count, columns // 2), F32), pltpu.VMEM(held.shape, held.dtype)],
+        [shape((2, new_count, columns // 2), F32), *[pltpu.VMEM(half_shape, held.dtype)] * 2],
         [attended, held, w_out],
         12,
-        scratch=[pltpu.SemaphoreType.DMA((COPIES,))],
+        scratch=[pltpu.SemaphoreType.DMA((2, COPIES))],
         hbm_in=1,
         cost=cost(2 * new_count * depth * columns, 2 * depth * columns),
     )
 
-    def project_more(own, name):
+    def project_more(own, name, weight):
         return call(
             lambda *refs: project_more_kernel(tile, own, *refs),
             name,
             [shape((new_count, columns // 2), F32)],
-            [attended_other, held_other, partial],
+            [attended_other, weight, partial],
             12,
             cost=cost(new_count * depth * columns, depth * columns),
         )[0]
 
-    sent = swap(project_more(False, "project_sent"), "tensor", 1)
-    half = project_more(True, "project_own") + sent
+    sent = swap(project_more(False, "project_sent", held_sent), "tensor", 1)
+    half = project_more(True, "project_own", held_kept) + sent
     quarter = half.shape[1] // 2
     low, high = half[:, :quarter], half[:, quarter:]
     upper = chip_at == 1
     arrived = swap(jnp.where(upper, low, high), "tensor", 2)
     summed = (jnp.where(upper, high, low) + arrived).astype(BF16)
 
-    def reply(order):
-        def run(value):
-            pairs = [(p * 4 + t, r * 4 + t) for r, p in enumerate(order) for t in range(4)]
-            crossed = [(source, target ^ 2) for source, target in pairs]
-            axes = ("rep", "tensor")
-            return lax.ppermute(value, axes, pairs), lax.ppermute(value, axes, crossed)
-
-        return run
-
-    summed, summed_across = lax.switch(index[0], [reply(o) for o in orders], summed)
+    summed = route(summed, index[0], orders, True)
+    summed_across = swap(summed, "tensor", 2)
     half = jnp.where(
         upper,
         jnp.concatenate([summed_across, summed], axis=1),

time: 77.6 us -> 69.8 us (0.90)
  starting transfers between devices: 26.4 us -> 18.7 us
  local copies, waits for them, and re-layouts: 5.14 us -> 4.21 us
    ppermute x2 -> x1, waiting for transfers between devices: 7.61 us -> 2.59 us  [branch(): return lambda v: lax.ppermute(v, 'rep', route_pairs(order, back))]
    ppermute x8 -> x9, waiting for transfers between devices: 10.5 us -> 14.1 us  [swap(): return lax.ppermute(value, axis, pairs)]
    ppermute x8 -> x9, starting transfers between devices: 8.9 us -> 5.6 us  [swap(): return lax.ppermute(value, axis, pairs)]
    ppermute x2 -> x1, starting transfers between devices: 7.13 us -> 4.5 us  [branch(): return lambda v: lax.ppermute(v, 'rep', route_pairs(order, back))]
    ppermute x1, waiting for transfers between devices: 3.41 us -> 5.32 us  [run(): lax.ppermute(query, 'rep', route_pairs(order, False))]
    ppermute x1, starting transfers between devices: 4.48 us -> 3.47 us  [run(): lax.ppermute(query, 'rep', route_pairs(order, False))]
    unnamed x6, local copies, waits for them, and re-layouts: 5.14 us -> 4.21 us
    ppermute x3, starting transfers between devices: 5.9 us -> 5.09 us  [cross(): return lax.ppermute(value, ('seq', 'tensor'), pairs)]
  transfers between devices with their start and end apart: 14 -> 14, of which waited for: 8 -> 6; matrix products, arithmetic and copies ran while one was open for 0% -> 0% of each run, Pallas kernels for 17% -> 19%
where the time goes in v1:
time: 69.8 us; the launch traced here: 69 us
  waiting for transfers between devices  22 us (32%)
  Pallas kernels  20.9 us (30%)
  starting transfers between devices  18.7 us (27%)
  local copies, waits for them, and re-layouts  4.21 us (6%)
  other arithmetic  2.11 us (3%)
  between operations  0.84 us (1%)
    pallas_call x8, Pallas kernels, call(): pl.pallas_call(body, out_shape=outs, in_specs=specs, out_specs=out_specs,...  20.9 us
    ppermute x9, waiting for transfers between devices, swap(): return lax.ppermute(value, axis, pairs)  14.1 us
    ppermute x9, starting transfers between devices, swap(): return lax.ppermute(value, axis, pairs)  5.6 us
    ppermute x1, waiting for transfers between devices, run(): lax.ppermute(query, 'rep', route_pairs(order, False))  5.32 us
    ppermute x3, starting transfers between devices, cross(): return lax.ppermute(value, ('seq', 'tensor'), pairs)  5.09 us
    ppermute x1, starting transfers between devices, branch(): return lambda v: lax.ppermute(v, 'rep', route_pairs(order, back))  4.5 us
    unnamed x6, local copies, waits for them, and re-layouts  4.21 us
    ppermute x1, starting transfers between devices, run(): lax.ppermute(query, 'rep', route_pairs(order, False))  3.47 us
  transfers between devices with their start and end apart: 14, of which 6 were waited for; matrix products, arithmetic and copies ran while one was open for 0% of the time, Pallas kernels for 19%

profile of v1, /device:TPU:0, one launch (start us, length us, event | category | flops | bytes accessed | tf_op | source)
XLA Modules:
  0.0 69.0 jit_solution(9040112454899696991)
XLA Ops:
  0.0 0.0 copy-start.2
  0.0 3.8 %compress.1 = (bf16[384,512]{1,0:T(8,128)(2,1)S(1)}, bf16[512,128]{1,0:T(8,128)(2,1)S(1)}, s32[1]{0:T(128)}) custom-call(s32[4]{0:T(128)} %refs_0_.1, bf16[1,384,8,256]{3,2,1,0:T(8,128)(2,1)} %refs_1_.1, bf16[2048,512]{1,0:T(8,128)(2,1)} %refs_2_.4, bf16[512]{0:T(512)(128)(2,1)} %refs_3_.1, bf16[1,64,16,128]{3,2,1,0:T(8,128)(2,1)} %refs_4_.3), custom_call_target="tpu_custom_call" | custom-call | flops 805306368 | bytes 1572864 | tf_op jit(solution)/shard_map/compress/pallas_call | solution.py:33
  4.4 13.6 %conditional.2 = (bf16[384,512]{1,0:T(8,128)(2,1)}, bf16[384,512]{1,0:T(8,128)(2,1)}, bf16[384,512]{1,0:T(8,128)(2,1)}, bf16[512,128]{1,0:T(8,128)(2,1)}) conditional(s32[]{:T(128)} %bitcast, (bf16[384,512]{1,0:T(8,128)(2,1)S(1)}, bf16[512,128]{1,0:T(8,128)(2,1)S(1)}) %tuple.174, (bf16[384,512]{1,0:T(8,128)(2,1)S(1)}, ...), branch_computations={%region_0.1_spmd, %region_1.2_spmd, %region_2.3_spmd, %region_3.4_... | conditional | bytes 5243072 | solution.py:320
  4.4 3.0 %collective-permute-start.32 = (bf16[384,512]{1,0:T(8,128)(2,1)S(1)}, bf16[384,512]{1,0:T(8,128)(2,1)}, u32[]{:S(2)}, u32[]{:S(2)}) collective-permute-start(bf16[384,512]{1,0:T(8,128)(2,1)S(1)} %get-tuple-element.166), channel_id=1, source_target_pairs={{0,16},{1,3},{2,18},{3,1},{16,0},{17,19},{18,2},{19,17},{4,20},{5,... | collective-permute-start | bytes 1179656 | tf_op jit(solution)/shard_map/cond/branch_8_fun/ppermute | solution.py:88
  7.5 1.5 %collective-permute-start.33 = (bf16[384,512]{1,0:T(8,128)(2,1)S(1)}, bf16[384,512]{1,0:T(8,128)(2,1)}, u32[]{:S(2)}, u32[]{:S(2)}) collective-permute-start(bf16[384,512]{1,0:T(8,128)(2,1)S(1)} %get-tuple-element.166), channel_id=1, source_target_pairs={{0,2},{1,17},{2,0},{3,19},{16,18},{17,1},{18,16},{19,3},{4,6},{5,2... | collective-permute-start | bytes 1179656 | tf_op jit(solution)/shard_map/cond/branch_8_fun/ppermute | solution.py:88
  9.0 0.0 collective-permute-start.34
  9.0 3.5 %collective-permute-start.35 = (bf16[512,128]{1,0:T(8,128)(2,1)S(1)}, bf16[512,128]{1,0:T(8,128)(2,1)}, u32[]{:S(2)}, u32[]{:S(2)}) collective-permute-start(bf16[512,128]{1,0:T(8,128)(2,1)S(1)} %get-tuple-element.167), channel_id=1, source_target_pairs={{0,4},{4,8},{8,0},{12,12},{1,5},{5,9},{9,1},{13,13},{2,6},{6,10},{... | collective-permute-start | bytes 393224 | tf_op jit(solution)/shard_map/cond/branch_8_fun/ppermute | solution.py:315
  12.5 5.3 %collective-permute-done.35 = bf16[512,128]{1,0:T(8,128)(2,1)} collective-permute-done((bf16[512,128]{1,0:T(8,128)(2,1)S(1)}, bf16[512,128]{1,0:T(8,128)(2,1)}, u32[]{:S(2)}, u32[]{:S(2)}) %collective-permute-start.35) | collective-permute-done | bytes 131104 | tf_op jit(solution)/shard_map/cond/branch_8_fun/ppermute | solution.py:315
  17.8 0.0 collective-permute-done.32
  17.8 0.0 collective-permute-done.33
  17.8 0.0 collective-permute-done.34
  18.0 0.1 collective-permute-start.121
  18.1 0.5 collective-permute-start.122
  18.6 0.6 collective-permute-start.120
  19.1 0.0 copy-done.2
  19.1 5.1 %score_chip.1 = (f32[768,512]{1,0:T(8,128)S(1)}, bf16[768,128]{1,0:T(8,128)(2,1)S(1)}, f32[8,512]{1,0:T(8,128)S(1)}, bf16[1024,4096]{1,0:T(8,128)(2,1)S(1)}) custom-call(bf16[384,512]{1,0:T(8,128)(2,1)S(1)} %get-tuple-element.222.refs_0_, bf16[384,512]{1,0:T(8,128)(2,1)} %get-tuple-element.224.refs_1_, bf16[2,512,256]{2,1,0:T(8,128)(2,1)S(1)} %copy-done.2, ...), custom_call_target="tpu_custom_call" | custom-call | flops 301989888 | bytes 8388608 | tf_op jit(solution)/shard_map/score_chip/pallas_call | solution.py:33
  24.2 0.0 collective-permute-done.121.refs_1_
  24.2 0.0 collective-permute-done.122.refs_3_
  24.2 2.3 %score_next.1 = (f32[1536,512]{1,0:T(8,128)S(1)}, bf16[1536,128]{1,0:T(8,128)(2,1)S(1)}, f32[8,512]{1,0:T(8,128)S(1)}) custom-call(bf16[384,512]{1,0:T(8,128)(2,1)} %get-tuple-element.228.refs_0_, bf16[384,512]{1,0:T(8,128)(2,1)S(1)} %collective-permute-done.121.refs_1_, bf16[384,512]{1,0:T(8,128)(2,1)} %get-tuple-element.230.refs_2_, ...), custom_call_target="tpu_custom_call" | custom-call | flops 603979776 | bytes 4718592 | tf_op jit(solution)/shard_map/score_next/pallas_call | solution.py:33
  26.6 0.0 collective-permute-done.120.refs_0_
  26.6 0.8 %collective-permute-start.123 = (bf16[384,512]{1,0:T(8,128)(2,1)S(1)}, bf16[384,512]{1,0:T(8,128)(2,1)S(1)}, u32[]{:S(2)}, u32[]{:S(2)}) collective-permute-start(bf16[384,512]{1,0:T(8,128)(2,1)S(1)} %collective-permute-done.120.refs_0_), channel_id=1, source_target_pairs={{0,1},{1,0},{2,3},{3,2},{4,5},{5,4},{6,7},{7,6},{8,9},{9,8},{10,11... | collective-permute-start | bytes 1179656 | tf_op jit(solution)/shard_map/ppermute | solution.py:83
  27.4 1.3 %collective-permute-done.123.refs_1_ = bf16[384,512]{1,0:T(8,128)(2,1)S(1)} collective-permute-done((bf16[384,512]{1,0:T(8,128)(2,1)S(1)}, bf16[384,512]{1,0:T(8,128)(2,1)S(1)}, u32[]{:S(2)}, u32[]{:S(2)}) %collective-permute-start.123) | collective-permute-done | bytes 393248 | tf_op jit(solution)/shard_map/ppermute | solution.py:83
  28.8 1.7 %score_corner.1 = (f32[768,512]{1,0:T(8,128)S(1)}, bf16[768,128]{1,0:T(8,128)(2,1)S(1)}, f32[8,512]{1,0:T(8,128)S(1)}) custom-call(bf16[384,512]{1,0:T(8,128)(2,1)S(1)} %collective-permute-done.120.refs_0_, bf16[384,512]{1,0:T(8,128)(2,1)S(1)} %collective-permute-done.123.refs_1_, bf16[2,512,256]{2,1,0:T(8,128)(2,1)S(1)} %copy-done.2, ...), custom_call_target="tpu_custom_call" | custom-call | flops 301989888 | bytes 2359296 | tf_op jit(solution)/shard_map/score_corner/pallas_call | solution.py:33
  30.5 1.4 %attend.1.refs_0_ = bf16[64,1024]{1,0:T(8,128)(2,1)S(1)} custom-call(f32[768,512]{1,0:T(8,128)S(1)} %get-tuple-element.226.refs_0_, bf16[768,128]{1,0:T(8,128)(2,1)S(1)} %get-tuple-element.227.refs_1_, f32[8,512]{1,0:T(8,128)S(1)} %get-tuple-element.232.refs_2_, f32[1536,512]{1,0:T(8,128)S(1)} %get-tuple-element.233.refs_3_, ...), custom_call_target="tpu_custom_call" | custom-call | flops 402653184 | bytes 6291456 | tf_op jit(solution)/shard_map/attend/pallas_call | solution.py:33
  31.9 1.3 %collective-permute-start.124 = (bf16[64,1024]{1,0:T(8,128)(2,1)S(1)}, bf16[64,1024]{1,0:T(8,128)(2,1)S(1)}, u32[]{:S(2)}, u32[]{:S(2)}) collective-permute-start(bf16[64,1024]{1,0:T(8,128)(2,1)S(1)} %attend.1.refs_0_), channel_id=1, source_target_pairs={{0,16},{16,0},{1,17},{17,1},{2,18},{18,2},{3,19},{19,3},{4,20},{20... | collective-permute-start | bytes 393224 | tf_op jit(solution)/shard_map/ppermute | solution.py:83
  33.2 4.9 %project.1 = (f32[2,64,2048]{2,1,0:T(8,128)S(1)}, bf16[1024,2048]{1,0:T(8,128)(2,1)S(1)}, bf16[1024,2048]{1,0:T(8,128)(2,1)S(1)}) custom-call(bf16[64,1024]{1,0:T(8,128)(2,1)S(1)} %attend.1.refs_0_, bf16[1024,4096]{1,0:T(8,128)(2,1)S(1)} %get-tuple-element.240.refs_1_, bf16[2048,4096]{1,0:T(8,128)(2,1)} %refs_2_.7), custom_call_target="tpu_custom_call" | custom-call | flops 536870912 | bytes 8388608 | tf_op jit(solution)/shard_map/project/pallas_call | solution.py:33
  38.2 0.0 copy-start
  38.2 2.0 %copy-done = bf16[1024,2048]{1,0:T(8,128)(2,1)} copy-done((bf16[1024,2048]{1,0:T(8,128)(2,1)}, bf16[1024,2048]{1,0:T(8,128)(2,1)S(1)}, u32[]{:S(2)}) %copy-start) | copy-done | bytes 4194328
  40.2 0.0 collective-permute-done.124.refs_0_
  40.2 0.8 %project_sent.1 = f32[64,2048]{1,0:T(8,128)S(1)} custom-call(bf16[64,1024]{1,0:T(8,128)(2,1)S(1)} %collective-permute-done.124.refs_0_, bf16[1024,2048]{1,0:T(8,128)(2,1)S(1)} %get-tuple-element.243.refs_1_, f32[2,64,2048]{2,1,0:T(8,128)S(1)} %get-tuple-element.242.refs_2_), custom_call_target="tpu_custom_call" | custom-call | flops 268435456 | bytes 4194304 | tf_op jit(solution)/shard_map/project_sent/pallas_call | solution.py:33
  41.0 0.1 collective-permute-start.125
  41.1 0.0 copy-start.1
  41.1 2.2 %copy-done.1 = bf16[1024,2048]{1,0:T(8,128)(2,1)S(1)} copy-done((bf16[1024,2048]{1,0:T(8,128)(2,1)S(1)}, bf16[1024,2048]{1,0:T(8,128)(2,1)}, u32[]{:S(2)}) %copy-start.1) | copy-done | bytes 4194328
  43.3 0.8 %project_own.1 = f32[64,2048]{1,0:T(8,128)S(1)} custom-call(bf16[64,1024]{1,0:T(8,128)(2,1)S(1)} %collective-permute-done.124.refs_0_, bf16[1024,2048]{1,0:T(8,128)(2,1)S(1)} %copy-done.1, f32[2,64,2048]{2,1,0:T(8,128)S(1)} %get-tuple-element.242.refs_2_), custom_call_target="tpu_custom_call" | custom-call | flops 268435456 | bytes 4194304 | tf_op jit(solution)/shard_map/project_own/pallas_call | solution.py:33
  44.2 0.0 collective-permute-done.125
  44.2 0.1 add.12
  44.3 1.4 %collective-permute-start.126 = (f32[64,1024]{1,0:T(8,128)S(1)}, f32[64,1024]{1,0:T(8,128)S(1)}, u32[]{:S(2)}, u32[]{:S(2)}) collective-permute-start(f32[64,1024]{1,0:T(8,128)S(1)} %slice_select_fusion), channel_id=1, source_target_pairs={{0,2},{1,3},{2,0},{3,1},{4,6},{5,7},{6,4},{7,5},{8,10},{9,11},{10,... | collective-permute-start | bytes 786440 | tf_op jit(solution)/shard_map/ppermute | solution.py:83
  45.7 7.4 %collective-permute-done.126 = f32[64,1024]{1,0:T(8,128)S(1)} collective-permute-done((f32[64,1024]{1,0:T(8,128)S(1)}, f32[64,1024]{1,0:T(8,128)S(1)}, u32[]{:S(2)}, u32[]{:S(2)}) %collective-permute-start.126) | collective-permute-done | bytes 262176 | tf_op jit(solution)/shard_map/ppermute | solution.py:83
  53.1 7.1 %conditional.3 = (bf16[64,1024]{1,0:T(8,128)(2,1)}) conditional(s32[]{:T(128)} %bitcast, bf16[64,1024]{1,0:T(8,128)(2,1)S(1)} %add_convert_fusion, bf16[64,1024]{1,0:T(8,128)(2,1)S(1)} %add_convert_fusion, bf16[64,1024]{1,0:T(8,128)(2,1)S(1)} %add_convert_fusion, bf16[64,1024]{1,0:T(8,128)(2,1)S(1)} %add_convert_fusion, ...), branch_computations={%region_24.25_spmd, %region_25.26_spmd, %region_26.27_spmd, %regio... | conditional | bytes 524336 | solution.py:73
  53.1 4.5 %collective-permute-start.104 = (bf16[64,1024]{1,0:T(8,128)(2,1)S(1)}, bf16[64,1024]{1,0:T(8,128)(2,1)}, u32[]{:S(2)}, u32[]{:S(2)}) collective-permute-start(bf16[64,1024]{1,0:T(8,128)(2,1)S(1)} %param.32), channel_id=1, source_target_pairs={{4,0},{8,4},{0,8},{12,12},{5,1},{9,5},{1,9},{13,13},{6,2},{10,6},{... | collective-permute-start | bytes 393224 | tf_op jit(solution)/shard_map/cond/branch_8_fun/ppermute | solution.py:71
  57.6 2.6 %collective-permute-done.104 = bf16[64,1024]{1,0:T(8,128)(2,1)} collective-permute-done((bf16[64,1024]{1,0:T(8,128)(2,1)S(1)}, bf16[64,1024]{1,0:T(8,128)(2,1)}, u32[]{:S(2)}, u32[]{:S(2)}) %collective-permute-start.104) | collective-permute-done | bytes 131104 | tf_op jit(solution)/shard_map/cond/branch_8_fun/ppermute | solution.py:71
  60.2 1.3 %collective-permute-start.127 = (bf16[64,1024]{1,0:T(8,128)(2,1)}, bf16[64,1024]{1,0:T(8,128)(2,1)S(1)}, u32[]{:S(2)}, u32[]{:S(2)}) collective-permute-start(bf16[64,1024]{1,0:T(8,128)(2,1)} %get-tuple-element.340), channel_id=1, source_target_pairs={{0,2},{1,3},{2,0},{3,1},{4,6},{5,7},{6,4},{7,5},{8,10},{9,11},{10,... | collective-permute-start | bytes 393224 | tf_op jit(solution)/shard_map/ppermute | solution.py:83
  61.6 3.8 %collective-permute-done.127 = bf16[64,1024]{1,0:T(8,128)(2,1)S(1)} collective-permute-done((bf16[64,1024]{1,0:T(8,128)(2,1)}, bf16[64,1024]{1,0:T(8,128)(2,1)S(1)}, u32[]{:S(2)}, u32[]{:S(2)}) %collective-permute-start.127) | collective-permute-done | bytes 131104 | tf_op jit(solution)/shard_map/ppermute | solution.py:83
  65.4 1.0 %maximum_select_fusion.1 = bf16[64,2048]{1,0:T(8,128)(2,1)S(1)} fusion(bf16[64,1024]{1,0:T(8,128)(2,1)} %get-tuple-element.340, bf16[64,1024]{1,0:T(8,128)(2,1)S(1)} %collective-permute-done.127, pred[]{:T(512)S(6)} %eq.9), kind=kLoop, calls=%fused_computation.1 | loop fusion | flops 1179648 | bytes 524289 | tf_op jit(solution)/shard_map/jit(_where)/select_n | solution.py:375
  66.4 0.1 collective-permute-start.128
  66.5 1.5 %collective-permute-done.128 = bf16[64,2048]{1,0:T(8,128)(2,1)S(1)} collective-permute-done((bf16[64,2048]{1,0:T(8,128)(2,1)S(1)}, bf16[64,2048]{1,0:T(8,128)(2,1)S(1)}, u32[]{:S(2)}, u32[]{:S(2)}) %collective-permute-start.128) | collective-permute-done | bytes 262176 | tf_op jit(solution)/shard_map/ppermute | solution.py:83
  68.0 0.9 %maximum_select_fusion = bf16[1,64,4096]{2,1,0:T(8,128)(2,1)} fusion(bf16[1,64,2048]{2,1,0:T(8,128)(2,1)S(1)} %bitcast.3, bf16[1,64,2048]{2,1,0:T(8,128)(2,1)S(1)} %bitcast.4, pred[]{:T(512)S(6)} %eq.8), kind=kLoop, calls=%fused_computation | loop fusion | flops 2359296 | bytes 1048577 | tf_op jit(solution)/shard_map/jit(_where)/select_n | solution.py:381
  (2 shorter events, 0.1 us)
Async XLA Ops:
  0.0 19.1 %copy-start.2 = (bf16[2,512,256]{2,1,0:T(8,128)(2,1)S(1)}, bf16[2,512,256]{2,1,0:T(8,128)(2,1)}, u32[]{:S(2)}) copy-start(bf16[2,512,256]{2,1,0:T(8,128)(2,1)} %refs_2_.6) | copy-start | bytes 1572868
  4.4 13.3 %collective-permute-start.32 = (bf16[384,512]{1,0:T(8,128)(2,1)S(1)}, bf16[384,512]{1,0:T(8,128)(2,1)}, u32[]{:S(2)}, u32[]{:S(2)}) collective-permute-start(bf16[384,512]{1,0:T(8,128)(2,1)S(1)} %get-tuple-element.166), channel_id=1, source_target_pairs={{0,16},{1,3},{2,18},{3,1},{16,0},{17,19},{18,2},{19,17},{4,20},{5,... | collective-permute-start | bytes 1179656 | tf_op jit(solution)/shard_map/cond/branch_8_fun/ppermute | solution.py:88
  7.5 10.3 %collective-permute-start.33 = (bf16[384,512]{1,0:T(8,128)(2,1)S(1)}, bf16[384,512]{1,0:T(8,128)(2,1)}, u32[]{:S(2)}, u32[]{:S(2)}) collective-permute-start(bf16[384,512]{1,0:T(8,128)(2,1)S(1)} %get-tuple-element.166), channel_id=1, source_target_pairs={{0,2},{1,17},{2,0},{3,19},{16,18},{17,1},{18,16},{19,3},{4,6},{5,2... | collective-permute-start | bytes 1179656 | tf_op jit(solution)/shard_map/cond/branch_8_fun/ppermute | solution.py:88
  9.0 8.8 %collective-permute-start.34 = (bf16[384,512]{1,0:T(8,128)(2,1)S(1)}, bf16[384,512]{1,0:T(8,128)(2,1)}, u32[]{:S(2)}, u32[]{:S(2)}) collective-permute-start(bf16[384,512]{1,0:T(8,128)(2,1)S(1)} %get-tuple-element.166), channel_id=1, source_target_pairs={{0,1},{1,0},{2,3},{3,2},{4,5},{5,4},{6,7},{7,6},{8,9},{9,8},{10,11... | collective-permute-start | bytes 1179656 | tf_op jit(solution)/shard_map/cond/branch_8_fun/ppermute | solution.py:83
  9.0 8.8 %collective-permute-start.35 = (bf16[512,128]{1,0:T(8,128)(2,1)S(1)}, bf16[512,128]{1,0:T(8,128)(2,1)}, u32[]{:S(2)}, u32[]{:S(2)}) collective-permute-start(bf16[512,128]{1,0:T(8,128)(2,1)S(1)} %get-tuple-element.167), channel_id=1, source_target_pairs={{0,4},{4,8},{8,0},{12,12},{1,5},{5,9},{9,1},{13,13},{2,6},{6,10},{... | collective-permute-start | bytes 393224 | tf_op jit(solution)/shard_map/cond/branch_8_fun/ppermute | solution.py:315
  18.0 6.2 %collective-permute-start.121 = (bf16[384,512]{1,0:T(8,128)(2,1)}, bf16[384,512]{1,0:T(8,128)(2,1)S(1)}, u32[]{:S(2)}, u32[]{:S(2)}) collective-permute-start(bf16[384,512]{1,0:T(8,128)(2,1)} %get-tuple-element.228.refs_0_), channel_id=1, source_target_pairs={{0,1},{1,0},{2,3},{3,2},{4,5},{5,4},{6,7},{7,6},{8,9},{9,8},{10,11... | collective-permute-start | bytes 1179656 | tf_op jit(solution)/shard_map/ppermute | solution.py:83
  18.1 6.2 %collective-permute-start.122 = (bf16[384,512]{1,0:T(8,128)(2,1)}, bf16[384,512]{1,0:T(8,128)(2,1)S(1)}, u32[]{:S(2)}, u32[]{:S(2)}) collective-permute-start(bf16[384,512]{1,0:T(8,128)(2,1)} %get-tuple-element.230.refs_2_), channel_id=1, source_target_pairs={{0,1},{1,0},{2,3},{3,2},{4,5},{5,4},{6,7},{7,6},{8,9},{9,8},{10,11... | collective-permute-start | bytes 1179656 | tf_op jit(solution)/shard_map/ppermute | solution.py:83
  18.6 8.0 %collective-permute-start.120 = (bf16[384,512]{1,0:T(8,128)(2,1)}, bf16[384,512]{1,0:T(8,128)(2,1)S(1)}, u32[]{:S(2)}, u32[]{:S(2)}) collective-permute-start(bf16[384,512]{1,0:T(8,128)(2,1)} %get-tuple-element.228.refs_0_), channel_id=1, source_target_pairs={{0,2},{1,17},{2,0},{3,19},{16,18},{17,1},{18,16},{19,3},{4,6},{5,2... | collective-permute-start | bytes 1179656 | tf_op jit(solution)/shard_map/ppermute | solution.py:88
  26.6 2.2 %collective-permute-start.123 = (bf16[384,512]{1,0:T(8,128)(2,1)S(1)}, bf16[384,512]{1,0:T(8,128)(2,1)S(1)}, u32[]{:S(2)}, u32[]{:S(2)}) collective-permute-start(bf16[384,512]{1,0:T(8,128)(2,1)S(1)} %collective-permute-done.120.refs_0_), channel_id=1, source_target_pairs={{0,1},{1,0},{2,3},{3,2},{4,5},{5,4},{6,7},{7,6},{8,9},{9,8},{10,11... | collective-permute-start | bytes 1179656 | tf_op jit(solution)/shard_map/ppermute | solution.py:83
  31.9 8.3 %collective-permute-start.124 = (bf16[64,1024]{1,0:T(8,128)(2,1)S(1)}, bf16[64,1024]{1,0:T(8,128)(2,1)S(1)}, u32[]{:S(2)}, u32[]{:S(2)}) collective-permute-start(bf16[64,1024]{1,0:T(8,128)(2,1)S(1)} %attend.1.refs_0_), channel_id=1, source_target_pairs={{0,16},{16,0},{1,17},{17,1},{2,18},{18,2},{3,19},{19,3},{4,20},{20... | collective-permute-start | bytes 393224 | tf_op jit(solution)/shard_map/ppermute | solution.py:83
  38.2 2.0 %copy-start = (bf16[1024,2048]{1,0:T(8,128)(2,1)}, bf16[1024,2048]{1,0:T(8,128)(2,1)S(1)}, u32[]{:S(2)}) copy-start(bf16[1024,2048]{1,0:T(8,128)(2,1)S(1)} %get-tuple-element.241.refs_1_) | copy-start | bytes 12582916
  41.0 3.1 %collective-permute-start.125 = (f32[64,2048]{1,0:T(8,128)S(1)}, f32[64,2048]{1,0:T(8,128)S(1)}, u32[]{:S(2)}, u32[]{:S(2)}) collective-permute-start(f32[64,2048]{1,0:T(8,128)S(1)} %project_sent.1), channel_id=1, source_target_pairs={{0,1},{1,0},{2,3},{3,2},{4,5},{5,4},{6,7},{7,6},{8,9},{9,8},{10,11... | collective-permute-start | bytes 1572872 | tf_op jit(solution)/shard_map/ppermute | solution.py:83
  41.1 2.2 %copy-start.1 = (bf16[1024,2048]{1,0:T(8,128)(2,1)S(1)}, bf16[1024,2048]{1,0:T(8,128)(2,1)}, u32[]{:S(2)}) copy-start(bf16[1024,2048]{1,0:T(8,128)(2,1)} %copy-done) | copy-start | bytes 12582916
  44.3 8.8 %collective-permute-start.126 = (f32[64,1024]{1,0:T(8,128)S(1)}, f32[64,1024]{1,0:T(8,128)S(1)}, u32[]{:S(2)}, u32[]{:S(2)}) collective-permute-start(f32[64,1024]{1,0:T(8,128)S(1)} %slice_select_fusion), channel_id=1, source_target_pairs={{0,2},{1,3},{2,0},{3,1},{4,6},{5,7},{6,4},{7,5},{8,10},{9,11},{10,... | collective-permute-start | bytes 786440 | tf_op jit(solution)/shard_map/ppermute | solution.py:83
  53.1 7.1 %collective-permute-start.104 = (bf16[64,1024]{1,0:T(8,128)(2,1)S(1)}, bf16[64,1024]{1,0:T(8,128)(2,1)}, u32[]{:S(2)}, u32[]{:S(2)}) collective-permute-start(bf16[64,1024]{1,0:T(8,128)(2,1)S(1)} %param.32), channel_id=1, source_target_pairs={{4,0},{8,4},{0,8},{12,12},{5,1},{9,5},{1,9},{13,13},{6,2},{10,6},{... | collective-permute-start | bytes 393224 | tf_op jit(solution)/shard_map/cond/branch_8_fun/ppermute | solution.py:71
  60.2 5.2 %collective-permute-start.127 = (bf16[64,1024]{1,0:T(8,128)(2,1)}, bf16[64,1024]{1,0:T(8,128)(2,1)S(1)}, u32[]{:S(2)}, u32[]{:S(2)}) collective-permute-start(bf16[64,1024]{1,0:T(8,128)(2,1)} %get-tuple-element.340), channel_id=1, source_target_pairs={{0,2},{1,3},{2,0},{3,1},{4,6},{5,7},{6,4},{7,5},{8,10},{9,11},{10,... | collective-permute-start | bytes 393224 | tf_op jit(solution)/shard_map/ppermute | solution.py:83
  66.4 1.6 %collective-permute-start.128 = (bf16[64,2048]{1,0:T(8,128)(2,1)S(1)}, bf16[64,2048]{1,0:T(8,128)(2,1)S(1)}, u32[]{:S(2)}, u32[]{:S(2)}) collective-permute-start(bf16[64,2048]{1,0:T(8,128)(2,1)S(1)} %maximum_select_fusion.1), channel_id=1, source_target_pairs={{0,1},{1,0},{2,3},{3,2},{4,5},{5,4},{6,7},{7,6},{8,9},{9,8},{10,11... | collective-permute-start | bytes 786440 | tf_op jit(solution)/shard_map/ppermute | solution.py:83

commit v2 on v1

--- a/solution.py
+++ b/solution.py
@@ -171,50 +171,38 @@
     top_ref[...] = jnp.broadcast_to(top, top_ref.shape)
 
 
-def weight_copies(own, core, weight_ref, held_ref, sems):
-    depth, columns = held_ref.shape
+def fetch_kernel(weight_ref, own_ref, sent_ref, kept_ref, sems):
+    core = lax.axis_index("tensor") % 2
+    depth, columns = sent_ref.shape
     rows = depth // COPIES
-    half = lax.axis_index("seq") if own else 1 - lax.axis_index("seq")
-    first = 0 if core is None else core * columns
+    group = lax.axis_index("seq")
     copies = []
-    for i in range(COPIES):
-        start = pl.multiple_of(half * depth + i * rows, rows)
-        source = weight_ref.at[pl.ds(start, rows), pl.ds(pl.multiple_of(first, columns), columns)]
-        copies.append(
-            pltpu.make_async_copy(source, held_ref.at[pl.ds(i * rows, rows)], sems.at[i])
-        )
-    return copies
-
-
-def score_and_fetch_kernel(parts, *refs):
-    *refs, held_ref, sems = refs
-    copies = weight_copies(True, None, refs.pop(parts + 2), held_ref, sems)
+    for part, (held_ref, half, first) in enumerate(
+        ((own_ref, group, 0), (sent_ref, 1 - group, 1 - core), (kept_ref, 1 - group, core))
+    ):
+        first = pl.multiple_of(first * columns, columns)
+        for i in range(COPIES):
+            start = pl.multiple_of(half * depth + i * rows, rows)
+            source = weight_ref.at[pl.ds(start, rows), pl.ds(first, held_ref.shape[1])]
+            target = held_ref.at[pl.ds(i * rows, rows)]
+            copies.append(pltpu.make_async_copy(source, target, sems.at[part, i]))
     for copy in copies:
         copy.start()
-    score_kernel(parts, *refs)
     for copy in copies:
         copy.wait()
 
 
-def score_call(name, latents, lift, query, weight=None):
+def score_call(name, latents, lift, query):
     tokens = sum(latent.shape[0] for latent in latents)
     rows, head_size = query.shape
     flops = 2 * tokens * (lift.shape[1] * lift.shape[2] + rows * head_size)
-    outs = [shape((tokens, rows), F32), shape((tokens, head_size), BF16), shape((8, rows), F32)]
-    operands = [*latents, lift, query]
-    if weight is None:
-        body = lambda *refs: score_kernel(len(latents), *refs)
-        return call(body, name, outs, operands, 16, cost=cost(flops, 6 * tokens * rows))
-    held = (weight.shape[0] // 2, weight.shape[1])
     return call(
-        lambda *refs: score_and_fetch_kernel(len(latents), *refs),
+        lambda *refs: score_kernel(len(latents), *refs),
         name,
-        [*outs, pltpu.VMEM(held, weight.dtype)],
-        [*operands, weight],
+        [shape((tokens, rows), F32), shape((tokens, head_size), BF16), shape((8, rows), F32)],
+        [*latents, lift, query],
         16,
-        scratch=[pltpu.SemaphoreType.DMA((COPIES,))],
-        hbm_in=1,
-        cost=cost(flops, 2 * held[0] * held[1]),
+        cost=cost(flops, 6 * tokens * rows),
     )
 
 
@@ -244,12 +232,7 @@
         ].astype(BF16)
 
 
-def project_kernel(tile, rows_ref, weight_ref, all_ref, out_ref, sent_ref, kept_ref, sems):
-    core = lax.axis_index("tensor") % 2
-    copies = weight_copies(False, 1 - core, all_ref, sent_ref, sems.at[0])
-    copies += weight_copies(False, core, all_ref, kept_ref, sems.at[1])
-    for copy in copies:
-        copy.start()
+def project_kernel(tile, rows_ref, weight_ref, out_ref):
     rows = rows_ref[...]
     width = out_ref.shape[2]
     for part in range(out_ref.shape[0]):
@@ -258,8 +241,6 @@
             out_ref[part, :, column : column + tile] = dot(
                 rows, weight_ref[:, at : at + tile]
             )
-    for copy in copies:
-        copy.wait()
 
 
 def project_more_kernel(tile, own, rows_ref, weight_ref, before_ref, *refs):
@@ -306,23 +287,30 @@
         cost=cost(2 * tokens * all_groups * width * latent_width, 2 * tokens * all_groups * width),
     )
 
-    def branch(order):
-        def run(latent, query):
-            return (
-                cross(latent, 0),
-                cross(latent, 1),
-                swap(latent, "tensor", 1),
-                lax.ppermute(query, "rep", route_pairs(order, False)),
-            )
-
-        return run
-
-    near, far, beside, query = lax.switch(index[0], [branch(o) for o in orders], latent, query)
+    near = cross(latent, 0)
+    far = cross(latent, 1)
+    query = route(query, index[0], orders, False)
+    weight, query = lax.optimization_barrier((w_out, query))
+    held_shape = (w_out.shape[0] // 2, w_out.shape[1])
+    half_shape = (held_shape[0], held_shape[1] // 2)
+    held, held_sent, held_kept = call(
+        fetch_kernel,
+        "fetch",
+        [pltpu.VMEM(dims, w_out.dtype) for dims in (held_shape, half_shape, half_shape)],
+        [weight],
+        4,
+        scratch=[pltpu.SemaphoreType.DMA((3, COPIES))],
+        hbm_in=1,
+        cost=cost(0, 0),
+    )
+    near, far, held = lax.optimization_barrier((near, far, held))
     corner = cross(near, 1)
+    beside = swap(latent, "tensor", 1)
     near_beside = swap(near, "tensor", 1)
     far_beside = swap(far, "tensor", 1)
-    *first, held = score_call("score_chip", [latent, beside], w_up, query, w_out)
-    *second, = score_call("score_next", [near, near_beside, far, far_beside], w_up, query)
+    first = score_call("score_chip", [latent, beside], w_up, query)
+    second = score_call("score_next", [near, near_beside, far, far_beside], w_up, query)
+    first, second = list(first), list(second)
     corner, first[2], second[2] = lax.optimization_barrier((corner, first[2], second[2]))
     corner_beside = swap(corner, "tensor", 1)
     third = score_call("score_corner", [corner, corner_beside], w_up, query)
@@ -340,15 +328,12 @@
     attended_other = swap(attended, "seq", 1)
     columns = w_out.shape[1]
     tile = min(512, columns // 2)
-    half_shape = (held.shape[0], held.shape[1] // 2)
-    partial, held_sent, held_kept = call(
+    (partial,) = call(
         lambda *refs: project_kernel(tile, *refs),
         "project",
-        [shape((2, new_count, columns // 2), F32), *[pltpu.VMEM(half_shape, held.dtype)] * 2],
-        [attended, held, w_out],
+        [shape((2, new_count, columns // 2), F32)],
+        [attended, held],
         12,
-        scratch=[pltpu.SemaphoreType.DMA((2, COPIES))],
-        hbm_in=1,
         cost=cost(2 * new_count * depth * columns, 2 * depth * columns),
     )
 

time: 69.8 us -> 72.9 us (1.044)
  the two profiles are of different devices: /device:TPU:0 before, /device:TPU:17 now
where the time goes in v2:
time: 72.9 us; the launch traced here: 72.1 us
  waiting for transfers between devices  29.9 us (41%)
  Pallas kernels  19.8 us (27%)
  starting transfers between devices  15.2 us (21%)
  local copies, waits for them, and re-layouts  4.17 us (6%)
  other arithmetic  2.09 us (3%)
  between operations  0.79 us (1%)
    pallas_call x9, Pallas kernels, call(): pl.pallas_call(body, out_shape=outs, in_specs=specs, out_specs=out_specs,...  19.8 us
    ppermute x9, waiting for transfers between devices, swap(): return lax.ppermute(value, axis, pairs)  16.8 us
    ppermute x2, waiting for transfers between devices, branch(): return lambda v: lax.ppermute(v, 'rep', route_pairs(order, back))  10.2 us
    ppermute x9, starting transfers between devices, swap(): return lax.ppermute(value, axis, pairs)  8.5 us
    unnamed x6, local copies, waits for them, and re-layouts  4.17 us
    ppermute x2, starting transfers between devices, branch(): return lambda v: lax.ppermute(v, 'rep', route_pairs(order, back))  4 us
    ppermute x3, waiting for transfers between devices, cross(): return lax.ppermute(value, ('seq', 'tensor'), pairs)  2.86 us
    ppermute x3, starting transfers between devices, cross(): return lax.ppermute(value, ('seq', 'tensor'), pairs)  2.75 us
  transfers between devices with their start and end apart: 14, of which 8 were waited for; matrix products, arithmetic and copies ran while one was open for 0% of the time, Pallas kernels for 17%

profile of v2, /device:TPU:17, one launch (start us, length us, event | category | flops | bytes accessed | tf_op | source)
XLA Modules:
  0.0 72.1 jit_solution(989817066012606395)
XLA Ops:
  0.0 3.7 %compress.1 = (bf16[384,512]{1,0:T(8,128)(2,1)S(1)}, bf16[512,128]{1,0:T(8,128)(2,1)S(1)}, s32[1]{0:T(128)}) custom-call(s32[4]{0:T(128)} %refs_0_.1, bf16[1,384,8,256]{3,2,1,0:T(8,128)(2,1)} %refs_1_.1, bf16[2048,512]{1,0:T(8,128)(2,1)} %refs_2_.3, bf16[512]{0:T(512)(128)(2,1)} %refs_3_.1, bf16[1,64,16,128]{3,2,1,0:T(8,128)(2,1)} %refs_4_.2), custom_call_target="tpu_custom_call" | custom-call | flops 805306368 | bytes 1572864 | tf_op jit(solution)/shard_map/compress/pallas_call | solution.py:33
  3.7 1.3 %collective-permute-start.49 = (bf16[384,512]{1,0:T(8,128)(2,1)S(1)}, bf16[384,512]{1,0:T(8,128)(2,1)S(1)}, u32[]{:S(2)}, u32[]{:S(2)}) collective-permute-start(bf16[384,512]{1,0:T(8,128)(2,1)S(1)} %get-tuple-element.127.refs_0_), channel_id=1, source_target_pairs={{0,16},{1,3},{2,18},{3,1},{16,0},{17,19},{18,2},{19,17},{4,20},{5,... | collective-permute-start | bytes 1179656 | tf_op jit(solution)/shard_map/ppermute | solution.py:88
  5.0 1.2 %collective-permute-start.50 = (bf16[384,512]{1,0:T(8,128)(2,1)S(1)}, bf16[384,512]{1,0:T(8,128)(2,1)S(1)}, u32[]{:S(2)}, u32[]{:S(2)}) collective-permute-start(bf16[384,512]{1,0:T(8,128)(2,1)S(1)} %get-tuple-element.127.refs_0_), channel_id=1, source_target_pairs={{0,2},{1,17},{2,0},{3,19},{16,18},{17,1},{18,16},{19,3},{4,6},{5,2... | collective-permute-start | bytes 1179656 | tf_op jit(solution)/shard_map/ppermute | solution.py:88
  6.2 1.2 %collective-permute-start.48 = (bf16[384,512]{1,0:T(8,128)(2,1)S(1)}, bf16[384,512]{1,0:T(8,128)(2,1)S(1)}, u32[]{:S(2)}, u32[]{:S(2)}) collective-permute-start(bf16[384,512]{1,0:T(8,128)(2,1)S(1)} %get-tuple-element.127.refs_0_), channel_id=1, source_target_pairs={{0,1},{1,0},{2,3},{3,2},{4,5},{5,4},{6,7},{7,6},{8,9},{9,8},{10,11... | collective-permute-start | bytes 1179656 | tf_op jit(solution)/shard_map/ppermute | solution.py:83
  8.1 8.1 %conditional.2 = (bf16[512,128]{1,0:T(8,128)(2,1)}) conditional(s32[]{:T(128)} %bitcast, bf16[512,128]{1,0:T(8,128)(2,1)S(1)} %get-tuple-element.128, bf16[512,128]{1,0:T(8,128)(2,1)S(1)} %get-tuple-element.128, bf16[512,128]{1,0:T(8,128)(2,1)S(1)} %get-tuple-element.128, ...), branch_computations={%region_0.1_spmd, %region_1.2_spmd, %region_2.3_spmd, %region_3.4_... | conditional | bytes 524336 | solution.py:73
  8.1 2.1 %collective-permute-start.12 = (bf16[512,128]{1,0:T(8,128)(2,1)S(1)}, bf16[512,128]{1,0:T(8,128)(2,1)}, u32[]{:S(2)}, u32[]{:S(2)}) collective-permute-start(bf16[512,128]{1,0:T(8,128)(2,1)S(1)} %param.12), channel_id=1, source_target_pairs={{0,8},{4,0},{8,4},{12,12},{1,9},{5,1},{9,5},{13,13},{2,10},{6,2},{... | collective-permute-start | bytes 393224 | tf_op jit(solution)/shard_map/cond/branch_12_fun/ppermute | solution.py:71
  10.2 5.9 %collective-permute-done.12 = bf16[512,128]{1,0:T(8,128)(2,1)} collective-permute-done((bf16[512,128]{1,0:T(8,128)(2,1)S(1)}, bf16[512,128]{1,0:T(8,128)(2,1)}, u32[]{:S(2)}, u32[]{:S(2)}) %collective-permute-start.12) | collective-permute-done | bytes 131104 | tf_op jit(solution)/shard_map/cond/branch_12_fun/ppermute | solution.py:71
  16.2 0.0 copy-start.2
  16.2 6.0 %fetch.1 = (bf16[1024,4096]{1,0:T(8,128)(2,1)S(1)}, bf16[1024,2048]{1,0:T(8,128)(2,1)S(1)}, bf16[1024,2048]{1,0:T(8,128)(2,1)S(1)}) custom-call(bf16[2048,4096]{1,0:T(8,128)(2,1)} %weight_ref), custom_call_target="tpu_custom_call" | custom-call | tf_op jit(solution)/shard_map/fetch/pallas_call | solution.py:33
  22.2 0.0 copy-start
  22.2 2.0 %copy-done = bf16[1024,2048]{1,0:T(8,128)(2,1)} copy-done((bf16[1024,2048]{1,0:T(8,128)(2,1)}, bf16[1024,2048]{1,0:T(8,128)(2,1)S(1)}, u32[]{:S(2)}) %copy-start) | copy-done | bytes 4194328
  24.2 0.0 collective-permute-done.49.refs_0_
  24.2 0.0 collective-permute-done.50.refs_2_
  24.2 0.8 %collective-permute-start.52 = (bf16[384,512]{1,0:T(8,128)(2,1)S(1)}, bf16[384,512]{1,0:T(8,128)(2,1)S(1)}, u32[]{:S(2)}, u32[]{:S(2)}) collective-permute-start(bf16[384,512]{1,0:T(8,128)(2,1)S(1)} %collective-permute-done.49.refs_0_), channel_id=1, source_target_pairs={{0,1},{1,0},{2,3},{3,2},{4,5},{5,4},{6,7},{7,6},{8,9},{9,8},{10,11... | collective-permute-start | bytes 1179656 | tf_op jit(solution)/shard_map/ppermute | solution.py:83
  25.0 0.1 collective-permute-start.53
  25.0 0.2 collective-permute-start.51
  25.3 0.0 collective-permute-done.48.refs_1_
  25.3 0.0 copy-done.2
  25.3 1.7 %score_chip.1 = (f32[768,512]{1,0:T(8,128)S(1)}, bf16[768,128]{1,0:T(8,128)(2,1)S(1)}, f32[8,512]{1,0:T(8,128)S(1)}) custom-call(bf16[384,512]{1,0:T(8,128)(2,1)S(1)} %get-tuple-element.127.refs_0_, bf16[384,512]{1,0:T(8,128)(2,1)S(1)} %collective-permute-done.48.refs_1_, bf16[2,512,256]{2,1,0:T(8,128)(2,1)S(1)} %copy-done.2, ...), custom_call_target="tpu_custom_call" | custom-call | flops 301989888 | bytes 2359296 | tf_op jit(solution)/shard_map/score_chip/pallas_call | solution.py:33
  27.0 0.0 collective-permute-done.52.refs_1_
  27.0 0.0 collective-permute-done.53.refs_3_
  27.0 2.1 %score_next.1 = (f32[1536,512]{1,0:T(8,128)S(1)}, bf16[1536,128]{1,0:T(8,128)(2,1)S(1)}, f32[8,512]{1,0:T(8,128)S(1)}) custom-call(bf16[384,512]{1,0:T(8,128)(2,1)S(1)} %collective-permute-done.49.refs_0_, bf16[384,512]{1,0:T(8,128)(2,1)S(1)} %collective-permute-done.52.refs_1_, bf16[384,512]{1,0:T(8,128)(2,1)S(1)} %collective-permute-done.50.refs_2_, ...), custom_call_target="tpu_custom_call" | custom-call | flops 603979776 | bytes 4718592 | tf_op jit(solution)/shard_map/score_next/pallas_call | solution.py:33
  29.1 2.9 %collective-permute-done.51.refs_0_ = bf16[384,512]{1,0:T(8,128)(2,1)S(1)} collective-permute-done((bf16[384,512]{1,0:T(8,128)(2,1)S(1)}, bf16[384,512]{1,0:T(8,128)(2,1)S(1)}, u32[]{:S(2)}, u32[]{:S(2)}) %collective-permute-start.51) | collective-permute-done | bytes 393248 | tf_op jit(solution)/shard_map/ppermute | solution.py:88
  32.0 1.3 %collective-permute-start.54 = (bf16[384,512]{1,0:T(8,128)(2,1)S(1)}, bf16[384,512]{1,0:T(8,128)(2,1)S(1)}, u32[]{:S(2)}, u32[]{:S(2)}) collective-permute-start(bf16[384,512]{1,0:T(8,128)(2,1)S(1)} %collective-permute-done.51.refs_0_), channel_id=1, source_target_pairs={{0,1},{1,0},{2,3},{3,2},{4,5},{5,4},{6,7},{7,6},{8,9},{9,8},{10,11... | collective-permute-start | bytes 1179656 | tf_op jit(solution)/shard_map/ppermute | solution.py:83
  33.3 1.3 %collective-permute-done.54.refs_1_ = bf16[384,512]{1,0:T(8,128)(2,1)S(1)} collective-permute-done((bf16[384,512]{1,0:T(8,128)(2,1)S(1)}, bf16[384,512]{1,0:T(8,128)(2,1)S(1)}, u32[]{:S(2)}, u32[]{:S(2)}) %collective-permute-start.54) | collective-permute-done | bytes 393248 | tf_op jit(solution)/shard_map/ppermute | solution.py:83
  34.6 1.7 %score_corner.1 = (f32[768,512]{1,0:T(8,128)S(1)}, bf16[768,128]{1,0:T(8,128)(2,1)S(1)}, f32[8,512]{1,0:T(8,128)S(1)}) custom-call(bf16[384,512]{1,0:T(8,128)(2,1)S(1)} %collective-permute-done.51.refs_0_, bf16[384,512]{1,0:T(8,128)(2,1)S(1)} %collective-permute-done.54.refs_1_, bf16[2,512,256]{2,1,0:T(8,128)(2,1)S(1)} %copy-done.2, ...), custom_call_target="tpu_custom_call" | custom-call | flops 301989888 | bytes 2359296 | tf_op jit(solution)/shard_map/score_corner/pallas_call | solution.py:33
  36.3 1.4 %attend.1.refs_0_ = bf16[64,1024]{1,0:T(8,128)(2,1)S(1)} custom-call(f32[768,512]{1,0:T(8,128)S(1)} %get-tuple-element.130.refs_0_, bf16[768,128]{1,0:T(8,128)(2,1)S(1)} %get-tuple-element.131.refs_1_, f32[8,512]{1,0:T(8,128)S(1)} %get-tuple-element.138.refs_2_, f32[1536,512]{1,0:T(8,128)S(1)} %get-tuple-element.139.refs_3_, ...), custom_call_target="tpu_custom_call" | custom-call | flops 402653184 | bytes 6291456 | tf_op jit(solution)/shard_map/attend/pallas_call | solution.py:33
  37.7 0.3 collective-permute-start.55
  38.0 1.5 %project.1.refs_2_ = f32[2,64,2048]{2,1,0:T(8,128)S(1)} custom-call(bf16[64,1024]{1,0:T(8,128)(2,1)S(1)} %attend.1.refs_0_, bf16[1024,4096]{1,0:T(8,128)(2,1)S(1)} %get-tuple-element.147.refs_1_), custom_call_target="tpu_custom_call" | custom-call | flops 536870912 | bytes 8388608 | tf_op jit(solution)/shard_map/project/pallas_call | solution.py:33
  39.6 2.9 %collective-permute-done.55.refs_0_ = bf16[64,1024]{1,0:T(8,128)(2,1)S(1)} collective-permute-done((bf16[64,1024]{1,0:T(8,128)(2,1)S(1)}, bf16[64,1024]{1,0:T(8,128)(2,1)S(1)}, u32[]{:S(2)}, u32[]{:S(2)}) %collective-permute-start.55) | collective-permute-done | bytes 131104 | tf_op jit(solution)/shard_map/ppermute | solution.py:83
  42.5 0.8 %project_sent.1 = f32[64,2048]{1,0:T(8,128)S(1)} custom-call(bf16[64,1024]{1,0:T(8,128)(2,1)S(1)} %collective-permute-done.55.refs_0_, bf16[1024,2048]{1,0:T(8,128)(2,1)S(1)} %get-tuple-element.148.refs_1_, f32[2,64,2048]{2,1,0:T(8,128)S(1)} %project.1.refs_2_), custom_call_target="tpu_custom_call" | custom-call | flops 268435456 | bytes 4194304 | tf_op jit(solution)/shard_map/project_sent/pallas_call | solution.py:33
  43.3 1.3 %collective-permute-start.56 = (f32[64,2048]{1,0:T(8,128)S(1)}, f32[64,2048]{1,0:T(8,128)S(1)}, u32[]{:S(2)}, u32[]{:S(2)}) collective-permute-start(f32[64,2048]{1,0:T(8,128)S(1)} %project_sent.1), channel_id=1, source_target_pairs={{0,1},{1,0},{2,3},{3,2},{4,5},{5,4},{6,7},{7,6},{8,9},{9,8},{10,11... | collective-permute-start | bytes 1572872 | tf_op jit(solution)/shard_map/ppermute | solution.py:83
  44.6 0.0 copy-start.1
  44.6 2.2 %copy-done.1 = bf16[1024,2048]{1,0:T(8,128)(2,1)S(1)} copy-done((bf16[1024,2048]{1,0:T(8,128)(2,1)S(1)}, bf16[1024,2048]{1,0:T(8,128)(2,1)}, u32[]{:S(2)}) %copy-start.1) | copy-done | bytes 4194328
  46.8 0.8 %project_own.1 = f32[64,2048]{1,0:T(8,128)S(1)} custom-call(bf16[64,1024]{1,0:T(8,128)(2,1)S(1)} %collective-permute-done.55.refs_0_, bf16[1024,2048]{1,0:T(8,128)(2,1)S(1)} %copy-done.1, f32[2,64,2048]{2,1,0:T(8,128)S(1)} %project.1.refs_2_), custom_call_target="tpu_custom_call" | custom-call | flops 268435456 | bytes 4194304 | tf_op jit(solution)/shard_map/project_own/pallas_call | solution.py:33
  47.6 0.0 collective-permute-done.56
  47.6 0.1 add.12
  47.8 0.3 collective-permute-start.57
  48.1 7.6 %collective-permute-done.57 = f32[64,1024]{1,0:T(8,128)S(1)} collective-permute-done((f32[64,1024]{1,0:T(8,128)S(1)}, f32[64,1024]{1,0:T(8,128)S(1)}, u32[]{:S(2)}, u32[]{:S(2)}) %collective-permute-start.57) | collective-permute-done | bytes 262176 | tf_op jit(solution)/shard_map/ppermute | solution.py:83
  55.8 6.2 %conditional.3 = (bf16[64,1024]{1,0:T(8,128)(2,1)}) conditional(s32[]{:T(128)} %bitcast, bf16[64,1024]{1,0:T(8,128)(2,1)S(1)} %add_convert_fusion, bf16[64,1024]{1,0:T(8,128)(2,1)S(1)} %add_convert_fusion, bf16[64,1024]{1,0:T(8,128)(2,1)S(1)} %add_convert_fusion, bf16[64,1024]{1,0:T(8,128)(2,1)S(1)} %add_convert_fusion, ...), branch_computations={%region_24.25_spmd, %region_25.26_spmd, %region_26.27_spmd, %regio... | conditional | bytes 524336 | solution.py:73
  55.8 1.9 %collective-permute-start.36 = (bf16[64,1024]{1,0:T(8,128)(2,1)S(1)}, bf16[64,1024]{1,0:T(8,128)(2,1)}, u32[]{:S(2)}, u32[]{:S(2)}) collective-permute-start(bf16[64,1024]{1,0:T(8,128)(2,1)S(1)} %param.36), channel_id=1, source_target_pairs={{8,0},{0,4},{4,8},{12,12},{9,1},{1,5},{5,9},{13,13},{10,2},{2,6},{... | collective-permute-start | bytes 393224 | tf_op jit(solution)/shard_map/cond/branch_12_fun/ppermute | solution.py:71
  57.7 4.3 %collective-permute-done.36 = bf16[64,1024]{1,0:T(8,128)(2,1)} collective-permute-done((bf16[64,1024]{1,0:T(8,128)(2,1)S(1)}, bf16[64,1024]{1,0:T(8,128)(2,1)}, u32[]{:S(2)}, u32[]{:S(2)}) %collective-permute-start.36) | collective-permute-done | bytes 131104 | tf_op jit(solution)/shard_map/cond/branch_12_fun/ppermute | solution.py:71
  62.0 0.3 collective-permute-start.58
  62.3 3.7 %collective-permute-done.58 = bf16[64,1024]{1,0:T(8,128)(2,1)S(1)} collective-permute-done((bf16[64,1024]{1,0:T(8,128)(2,1)}, bf16[64,1024]{1,0:T(8,128)(2,1)S(1)}, u32[]{:S(2)}, u32[]{:S(2)}) %collective-permute-start.58) | collective-permute-done | bytes 131104 | tf_op jit(solution)/shard_map/ppermute | solution.py:83
  66.0 1.0 %maximum_select_fusion.1 = bf16[64,2048]{1,0:T(8,128)(2,1)S(1)} fusion(bf16[64,1024]{1,0:T(8,128)(2,1)} %get-tuple-element.150, bf16[64,1024]{1,0:T(8,128)(2,1)S(1)} %collective-permute-done.58, pred[]{:T(512)S(6)} %eq.9), kind=kLoop, calls=%fused_computation.1 | loop fusion | flops 1179648 | bytes 524289 | tf_op jit(solution)/shard_map/jit(_where)/select_n | solution.py:360
  67.1 2.9 %collective-permute-start.59 = (bf16[64,2048]{1,0:T(8,128)(2,1)S(1)}, bf16[64,2048]{1,0:T(8,128)(2,1)S(1)}, u32[]{:S(2)}, u32[]{:S(2)}) collective-permute-start(bf16[64,2048]{1,0:T(8,128)(2,1)S(1)} %maximum_select_fusion.1), channel_id=1, source_target_pairs={{0,1},{1,0},{2,3},{3,2},{4,5},{5,4},{6,7},{7,6},{8,9},{9,8},{10,11... | collective-permute-start | bytes 786440 | tf_op jit(solution)/shard_map/ppermute | solution.py:83
  70.0 1.2 %collective-permute-done.59 = bf16[64,2048]{1,0:T(8,128)(2,1)S(1)} collective-permute-done((bf16[64,2048]{1,0:T(8,128)(2,1)S(1)}, bf16[64,2048]{1,0:T(8,128)(2,1)S(1)}, u32[]{:S(2)}, u32[]{:S(2)}) %collective-permute-start.59) | collective-permute-done | bytes 262176 | tf_op jit(solution)/shard_map/ppermute | solution.py:83
  71.2 0.9 %maximum_select_fusion = bf16[1,64,4096]{2,1,0:T(8,128)(2,1)} fusion(bf16[1,64,2048]{2,1,0:T(8,128)(2,1)S(1)} %bitcast.3, bf16[1,64,2048]{2,1,0:T(8,128)(2,1)S(1)} %bitcast.4, pred[]{:T(512)S(6)} %eq.8), kind=kLoop, calls=%fused_computation | loop fusion | flops 2359296 | bytes 1048577 | tf_op jit(solution)/shard_map/jit(_where)/select_n | solution.py:366
  (2 shorter events, 0.1 us)
Async XLA Ops:
  3.7 20.5 %collective-permute-start.49 = (bf16[384,512]{1,0:T(8,128)(2,1)S(1)}, bf16[384,512]{1,0:T(8,128)(2,1)S(1)}, u32[]{:S(2)}, u32[]{:S(2)}) collective-permute-start(bf16[384,512]{1,0:T(8,128)(2,1)S(1)} %get-tuple-element.127.refs_0_), channel_id=1, source_target_pairs={{0,16},{1,3},{2,18},{3,1},{16,0},{17,19},{18,2},{19,17},{4,20},{5,... | collective-permute-start | bytes 1179656 | tf_op jit(solution)/shard_map/ppermute | solution.py:88
  5.0 19.2 %collective-permute-start.50 = (bf16[384,512]{1,0:T(8,128)(2,1)S(1)}, bf16[384,512]{1,0:T(8,128)(2,1)S(1)}, u32[]{:S(2)}, u32[]{:S(2)}) collective-permute-start(bf16[384,512]{1,0:T(8,128)(2,1)S(1)} %get-tuple-element.127.refs_0_), channel_id=1, source_target_pairs={{0,2},{1,17},{2,0},{3,19},{16,18},{17,1},{18,16},{19,3},{4,6},{5,2... | collective-permute-start | bytes 1179656 | tf_op jit(solution)/shard_map/ppermute | solution.py:88
  6.2 19.0 %collective-permute-start.48 = (bf16[384,512]{1,0:T(8,128)(2,1)S(1)}, bf16[384,512]{1,0:T(8,128)(2,1)S(1)}, u32[]{:S(2)}, u32[]{:S(2)}) collective-permute-start(bf16[384,512]{1,0:T(8,128)(2,1)S(1)} %get-tuple-element.127.refs_0_), channel_id=1, source_target_pairs={{0,1},{1,0},{2,3},{3,2},{4,5},{5,4},{6,7},{7,6},{8,9},{9,8},{10,11... | collective-permute-start | bytes 1179656 | tf_op jit(solution)/shard_map/ppermute | solution.py:83
  8.1 8.0 %collective-permute-start.12 = (bf16[512,128]{1,0:T(8,128)(2,1)S(1)}, bf16[512,128]{1,0:T(8,128)(2,1)}, u32[]{:S(2)}, u32[]{:S(2)}) collective-permute-start(bf16[512,128]{1,0:T(8,128)(2,1)S(1)} %param.12), channel_id=1, source_target_pairs={{0,8},{4,0},{8,4},{12,12},{1,9},{5,1},{9,5},{13,13},{2,10},{6,2},{... | collective-permute-start | bytes 393224 | tf_op jit(solution)/shard_map/cond/branch_12_fun/ppermute | solution.py:71
  16.2 9.1 %copy-start.2 = (bf16[2,512,256]{2,1,0:T(8,128)(2,1)S(1)}, bf16[2,512,256]{2,1,0:T(8,128)(2,1)}, u32[]{:S(2)}) copy-start(bf16[2,512,256]{2,1,0:T(8,128)(2,1)} %refs_2_.5) | copy-start | bytes 1572868
  22.2 2.0 %copy-start = (bf16[1024,2048]{1,0:T(8,128)(2,1)}, bf16[1024,2048]{1,0:T(8,128)(2,1)S(1)}, u32[]{:S(2)}) copy-start(bf16[1024,2048]{1,0:T(8,128)(2,1)S(1)} %get-tuple-element.146.refs_1_) | copy-start | bytes 12582916
  24.2 2.8 %collective-permute-start.52 = (bf16[384,512]{1,0:T(8,128)(2,1)S(1)}, bf16[384,512]{1,0:T(8,128)(2,1)S(1)}, u32[]{:S(2)}, u32[]{:S(2)}) collective-permute-start(bf16[384,512]{1,0:T(8,128)(2,1)S(1)} %collective-permute-done.49.refs_0_), channel_id=1, source_target_pairs={{0,1},{1,0},{2,3},{3,2},{4,5},{5,4},{6,7},{7,6},{8,9},{9,8},{10,11... | collective-permute-start | bytes 1179656 | tf_op jit(solution)/shard_map/ppermute | solution.py:83
  25.0 2.0 %collective-permute-start.53 = (bf16[384,512]{1,0:T(8,128)(2,1)S(1)}, bf16[384,512]{1,0:T(8,128)(2,1)S(1)}, u32[]{:S(2)}, u32[]{:S(2)}) collective-permute-start(bf16[384,512]{1,0:T(8,128)(2,1)S(1)} %collective-permute-done.50.refs_2_), channel_id=1, source_target_pairs={{0,1},{1,0},{2,3},{3,2},{4,5},{5,4},{6,7},{7,6},{8,9},{9,8},{10,11... | collective-permute-start | bytes 1179656 | tf_op jit(solution)/shard_map/ppermute | solution.py:83
  25.0 6.9 %collective-permute-start.51 = (bf16[384,512]{1,0:T(8,128)(2,1)S(1)}, bf16[384,512]{1,0:T(8,128)(2,1)S(1)}, u32[]{:S(2)}, u32[]{:S(2)}) collective-permute-start(bf16[384,512]{1,0:T(8,128)(2,1)S(1)} %collective-permute-done.49.refs_0_), channel_id=1, source_target_pairs={{0,2},{1,17},{2,0},{3,19},{16,18},{17,1},{18,16},{19,3},{4,6},{5,2... | collective-permute-start | bytes 1179656 | tf_op jit(solution)/shard_map/ppermute | solution.py:88
  32.0 2.6 %collective-permute-start.54 = (bf16[384,512]{1,0:T(8,128)(2,1)S(1)}, bf16[384,512]{1,0:T(8,128)(2,1)S(1)}, u32[]{:S(2)}, u32[]{:S(2)}) collective-permute-start(bf16[384,512]{1,0:T(8,128)(2,1)S(1)} %collective-permute-done.51.refs_0_), channel_id=1, source_target_pairs={{0,1},{1,0},{2,3},{3,2},{4,5},{5,4},{6,7},{7,6},{8,9},{9,8},{10,11... | collective-permute-start | bytes 1179656 | tf_op jit(solution)/shard_map/ppermute | solution.py:83
  37.7 4.8 %collective-permute-start.55 = (bf16[64,1024]{1,0:T(8,128)(2,1)S(1)}, bf16[64,1024]{1,0:T(8,128)(2,1)S(1)}, u32[]{:S(2)}, u32[]{:S(2)}) collective-permute-start(bf16[64,1024]{1,0:T(8,128)(2,1)S(1)} %attend.1.refs_0_), channel_id=1, source_target_pairs={{0,16},{16,0},{1,17},{17,1},{2,18},{18,2},{3,19},{19,3},{4,20},{20... | collective-permute-start | bytes 393224 | tf_op jit(solution)/shard_map/ppermute | solution.py:83
  43.3 4.3 %collective-permute-start.56 = (f32[64,2048]{1,0:T(8,128)S(1)}, f32[64,2048]{1,0:T(8,128)S(1)}, u32[]{:S(2)}, u32[]{:S(2)}) collective-permute-start(f32[64,2048]{1,0:T(8,128)S(1)} %project_sent.1), channel_id=1, source_target_pairs={{0,1},{1,0},{2,3},{3,2},{4,5},{5,4},{6,7},{7,6},{8,9},{9,8},{10,11... | collective-permute-start | bytes 1572872 | tf_op jit(solution)/shard_map/ppermute | solution.py:83
  44.6 2.2 %copy-start.1 = (bf16[1024,2048]{1,0:T(8,128)(2,1)S(1)}, bf16[1024,2048]{1,0:T(8,128)(2,1)}, u32[]{:S(2)}) copy-start(bf16[1024,2048]{1,0:T(8,128)(2,1)} %copy-done) | copy-start | bytes 12582916
  47.8 8.0 %collective-permute-start.57 = (f32[64,1024]{1,0:T(8,128)S(1)}, f32[64,1024]{1,0:T(8,128)S(1)}, u32[]{:S(2)}, u32[]{:S(2)}) collective-permute-start(f32[64,1024]{1,0:T(8,128)S(1)} %slice_select_fusion), channel_id=1, source_target_pairs={{0,2},{1,3},{2,0},{3,1},{4,6},{5,7},{6,4},{7,5},{8,10},{9,11},{10,... | collective-permute-start | bytes 786440 | tf_op jit(solution)/shard_map/ppermute | solution.py:83
  55.8 6.2 %collective-permute-start.36 = (bf16[64,1024]{1,0:T(8,128)(2,1)S(1)}, bf16[64,1024]{1,0:T(8,128)(2,1)}, u32[]{:S(2)}, u32[]{:S(2)}) collective-permute-start(bf16[64,1024]{1,0:T(8,128)(2,1)S(1)} %param.36), channel_id=1, source_target_pairs={{8,0},{0,4},{4,8},{12,12},{9,1},{1,5},{5,9},{13,13},{10,2},{2,6},{... | collective-permute-start | bytes 393224 | tf_op jit(solution)/shard_map/cond/branch_12_fun/ppermute | solution.py:71
  62.0 4.0 %collective-permute-start.58 = (bf16[64,1024]{1,0:T(8,128)(2,1)}, bf16[64,1024]{1,0:T(8,128)(2,1)S(1)}, u32[]{:S(2)}, u32[]{:S(2)}) collective-permute-start(bf16[64,1024]{1,0:T(8,128)(2,1)} %get-tuple-element.150), channel_id=1, source_target_pairs={{0,2},{1,3},{2,0},{3,1},{4,6},{5,7},{6,4},{7,5},{8,10},{9,11},{10,... | collective-permute-start | bytes 393224 | tf_op jit(solution)/shard_map/ppermute | solution.py:83
  67.1 4.1 %collective-permute-start.59 = (bf16[64,2048]{1,0:T(8,128)(2,1)S(1)}, bf16[64,2048]{1,0:T(8,128)(2,1)S(1)}, u32[]{:S(2)}, u32[]{:S(2)}) collective-permute-start(bf16[64,2048]{1,0:T(8,128)(2,1)S(1)} %maximum_select_fusion.1), channel_id=1, source_target_pairs={{0,1},{1,0},{2,3},{3,2},{4,5},{5,4},{6,7},{7,6},{8,9},{9,8},{10,11... | collective-permute-start | bytes 786440 | tf_op jit(solution)/shard_map/ppermute | solution.py:83
